TPU v7x, 256 devices: a whole 4x4x8 slice. The times are simulated.
256 devices in a mesh: lon: 16 (over x_hi, y, core), lat: 8 (over z), rep: 2 (over x_lo).
Axes of the slice: x: 4 (x_hi: 2, x_lo: 2; x = x_hi * 2 + x_lo), y: 4, z: 8, core: 2. Of those that a mesh axis runs over, the one named last changes fastest.
Arguments:
- fine_field: bfloat16 [4, 96, 384, 192], P('rep', 'lat', 'lon'), may hold values from -6 to 6
- fine_gain: float32 [192], replicated, may hold values from 0.1 to 1.9
- fine_qkv: bfloat16 [192, 576], replicated, may hold values from -0.4375 to 0.4375
- fine_proj: bfloat16 [192, 192], replicated, may hold values from -0.4375 to 0.4375
- fine_table: float32 [2, 16, 6, 3312], P('rep', 'lat'), may hold values from -6 to 6
- merge_gain: float32 [768], replicated, may hold values from 0.1 to 1.9
- merge_weight: bfloat16 [768, 384], replicated, may hold values from -0.21875 to 0.21875
- coarse_gain: float32 [384], replicated, may hold values from 0.1 to 1.9
- coarse_qkv: bfloat16 [384, 1152], replicated, may hold values from -0.3125 to 0.3125
- coarse_proj: bfloat16 [384, 384], replicated, may hold values from -0.3125 to 0.3125
- coarse_table: float32 [2, 8, 12, 3312], P('rep', 'lat'), may hold values from -6 to 6
- cotangent: bfloat16 [4, 48, 192, 384], P('rep', 'lat', 'lon'), may hold values from -6 to 6
Outputs:
- coarse_out: bfloat16 [4, 48, 192, 384], P('rep', 'lat', 'lon')
- field_grad: bfloat16 [4, 96, 384, 192], P('rep', 'lat', 'lon')
- fine_gain_grad: float32 [192], replicated
- fine_qkv_grad: float32 [192, 576], replicated
- fine_proj_grad: float32 [192, 192], replicated
- fine_table_grad: float32 [2, 16, 6, 3312], P('rep', 'lat')
- merge_gain_grad: float32 [768], replicated
- merge_weight_grad: float32 [768, 384], replicated
- coarse_gain_grad: float32 [384], replicated
- coarse_qkv_grad: float32 [384, 1152], replicated
- coarse_proj_grad: float32 [384, 384], replicated
- coarse_table_grad: float32 [2, 8, 12, 3312], P('rep', 'lat')
All inputs are finite; a program needn't handle non-finite values.
Results may differ from a plain program's by a relative error of at most 0.033.
Values may be sent and summed in bfloat16 or wider, within the bound.
No kernel may reach another device: no remote copies, remote signals or barrier semaphores. Data moves between devices by JAX's collectives and lax.ppermute only.
A program may use at most 192 MiB of HBM per device.

v0:
```python
import numpy as np
import jax
import jax.numpy as jnp
from jax import lax
from jax.experimental import pallas as pl
from jax.experimental.pallas import tpu as pltpu
from jax.sharding import PartitionSpec as P

F32, BF = jnp.float32, jnp.bfloat16
EPS = 1e-05
TOK, HALF, LANES = 144, 72, 256
POS, DIAG = 3312, 23
RUN = 6 * DIAG
HEAD = 32
NEG = -1e30
COARSE, FINE, TAB = 432, 80, 64
GRAIN = COARSE + FINE
WIDE = 3456
FINE_ROWS, COARSE_ROWS = 6 * TOK + 8, 12 * TOK + 8
VMEM_LIMIT = 24 * 1024 * 1024


def dot(a, b, ca, cb):
    return lax.dot_general(a, b, (((ca,), (cb,)), ((), ())), preferred_element_type=F32)


def mm(a, b):
    return dot(a, b, 1, 0)


def mm_t(a, b):
    return dot(a, b, 1, 1)


def t_mm(a, b):
    return dot(a, b, 0, 0)


def low(x):
    return x.astype(BF)


def split3(x):
    hi = low(x)
    rest = x - hi.astype(F32)
    mid = low(rest)
    return hi, mid, low(rest - mid.astype(F32))


def iota(shape, dim):
    return lax.broadcasted_iota(jnp.int32, shape, dim)


def div_const(x, n):
    return lax.shift_right_logical(x * (65536 // n + 1), 16)


def one_hot(target, count):
    return jnp.where(iota((target.shape[0], count), 1) == target, 1.0, 0.0).astype(BF)


def window_index(rows):
    r = iota((rows, 1), 0)
    z = div_const(r, 72)
    r = r - z * 72
    w = div_const(r, 6)
    return z, r - w * 6, w


def pad_keys(x):
    gap = jnp.zeros((128 - HALF, x.shape[1]), F32)
    return low(jnp.concatenate([x[:HALF], gap, x[HALF:], gap], axis=0))


def unpad_keys(x):
    return jnp.concatenate([x[:HALF], x[128 : 128 + HALF]], axis=0)


def norm(x):
    width = sum(p.shape[1] for p in x)
    mean = sum(jnp.sum(p, axis=1, keepdims=True) for p in x) * (1.0 / width)
    shifted = [p - mean for p in x]
    var = sum(jnp.sum(p * p, axis=1, keepdims=True) for p in shifted) * (1.0 / width)
    inv = lax.rsqrt(var + EPS)
    return [p * inv for p in shifted], inv


def norm_back(grad, gain, hat, inv):
    width = sum(p.shape[1] for p in grad)
    scaled = [g * a for g, a in zip(grad, gain)]
    first = sum(jnp.sum(s, axis=1, keepdims=True) for s in scaled) * (1.0 / width)
    second = sum(jnp.sum(s * n, axis=1, keepdims=True) for s, n in zip(scaled, hat)) * (1.0 / width)
    gains = [jnp.sum(g * n, axis=0, keepdims=True) for g, n in zip(grad, hat)]
    return [inv * (s - first - n * second) for s, n in zip(scaled, hat)], gains


def load_bias(ref, kind, rows):
    return jnp.concatenate([ref[kind, 0, rows], ref[kind, 1, rows]], axis=1)


def head_mask(width, slot):
    lane = iota((1, width), 1)
    return (lane >= slot * HEAD) & (lane < (slot + 1) * HEAD)


def only_head(x, slot):
    return x * jnp.where(head_mask(x.shape[1], slot), 1.0, 0.0).astype(BF)


def by_head(x, slots):
    return jnp.concatenate([only_head(x, slot) for slot in range(slots)], axis=0)


def own_columns(x, slots):
    out = x[:TOK]
    for slot in range(1, slots):
        out = jnp.where(head_mask(x.shape[1], slot), x[slot * TOK : (slot + 1) * TOK], out)
    return out


def probabilities(q_stack, keys, bias):
    e = jnp.exp(mm_t(q_stack, keys) + bias)
    return e * (1.0 / jnp.sum(e, axis=1, keepdims=True))


def tile_forward(q, keys, values, bias, slots):
    p = probabilities(by_head(q, slots), keys, bias)
    return own_columns(mm(low(p), values), slots)


def tile_both(q, keys, values, gmix, bias, bias_grad_to, slots):
    q_stack, g_stack = by_head(q, slots), by_head(gmix, slots)
    p = probabilities(q_stack, keys, bias)
    p_low = low(p)
    mixed = own_columns(mm(p_low, values), slots)
    gp = mm_t(g_stack, values)
    gs = p * (gp - jnp.sum(p * gp, axis=1, keepdims=True))
    bias_grad_to(gs)
    gs_low = low(gs)
    gq = own_columns(mm(gs_low, keys), slots)
    return mixed, gq, t_mm(gs_low, q_stack), t_mm(p_low, g_stack)


def put(ref, grain, start, value):
    at = 0
    while at < value.shape[0]:
        chunk, row = divmod(start + at, grain)
        n = min(grain - row, value.shape[0] - at)
        ref[chunk, row : row + n] = value[at : at + n]
        at += n


def split_halves(pack_ref, keep_ref, send_ref):
    core = lax.axis_index("lon") % 2
    for own in range(2):

        @pl.when(core == own)
        def _():
            keep_ref[...] = pack_ref[8 * own : 8 * own + 8]
            send_ref[...] = pack_ref[8 - 8 * own : 16 - 8 * own]


def get_chunk(sums, chunk, rows):
    mine, other, core = sums
    return jnp.where(core == chunk // 8, mine[chunk % 8, rows].astype(F32), other[chunk % 8, rows].astype(F32))


def get(sums, grain, base, start, count):
    parts, at = [], 0
    while at < count:
        chunk, row = divmod(start + at, grain)
        n = min(grain - row, count - at)
        parts.append(get_chunk(sums, chunk, slice(base + row, base + row + n)))
        at += n
    return parts[0] if len(parts) == 1 else jnp.concatenate(parts, axis=0)


def gain_rows(pieces):
    line = pieces[0] if len(pieces) == 1 else jnp.concatenate(pieces, axis=1)
    width = line.shape[1]
    if width % 128:
        line = jnp.concatenate([line, jnp.zeros((1, 128 - width % 128), F32)], axis=1)
    rows = [line[:, 128 * i : 128 * i + 128] for i in range(line.shape[1] // 128)]
    rows.append(jnp.zeros((16 - len(rows), 128), F32))
    return low(jnp.concatenate(rows, axis=0))


def diagonal_select(first):
    lane = iota((1, 256), 1)
    wq = first + lax.shift_right_logical(lane, 7)
    lane = lane & 127
    wk = div_const(lane, 6)
    hk = lane - wk * 6
    diagonal = wq - wk + 11
    low_half = jnp.where((lane < HALF) & (hk < 3), hk * DIAG + diagonal, -1)
    high_half = jnp.where((lane < HALF) & (hk >= 3), (hk - 3) * DIAG + diagonal + 128, -1)
    target = jnp.maximum(low_half, high_half)
    return jnp.where(iota((256, 256), 0) == target, 1.0, 0.0).astype(BF)


HALF_RUN = 3 * DIAG


def table_groups():
    return [(g, (g // 12) * 16 + ((g // 6) % 2) * 8 + g % 6) for g in range(24)]


def table_slice(table, start):
    n = min(128, POS - start)
    part = table[:, start : start + n]
    if n < 128:
        part = jnp.concatenate([part, jnp.zeros((part.shape[0], 128 - n), F32)], axis=1)
    return part


def expand_tables(at_end, kinds, u_ref):
    lane, sub = iota((8, 128), 1), iota((8, 128), 0)
    column = div_const(lane, 6)
    crossing = (sub >= 3) != (lane - column * 6 >= 3)
    outside = jnp.where(lane >= HALF, NEG, 0.0)
    lev_term = jnp.where(at_end[0], NEG, 0.0)
    lat_term = jnp.where(crossing, jnp.where(at_end[1], NEG, 0.0), 0.0)
    u_ref[...] = jnp.zeros(u_ref.shape, F32)
    base = 0
    for table, _, _ in kinds:
        heads = table.shape[0]
        for g, row in table_groups():
            for half in range(2):
                u_ref[half, pl.ds(base + row, heads, stride=32)] = table_slice(table, g * RUN + half * HALF_RUN)
        base += heads * 32
    u = jnp.concatenate([u_ref[0, :base], u_ref[1, :base]], axis=1)
    hi = low(u)
    mid = low(u - hi.astype(F32))
    for first in range(0, 12, 2):
        sel = diagonal_select(first)
        x = mm(hi, sel) + mm(mid, sel)
        base = 0
        for table, may_end, out_ref in kinds:
            same = outside + lat_term if may_end else outside
            terms = same, same + lev_term
            for n in range(table.shape[0]):
                for zq in range(2):
                    for zk in range(2):
                        at = base + zq * 16 + zk * 8
                        for k in range(2):
                            to = n * TOK + zq * HALF + (first + k) * 6
                            part = x[at : at + 8, 128 * k : 128 * k + 128]
                            out_ref[zk, to : to + 6] = (part + terms[zq != zk])[:6]
                base += 32


def fold_tables(types, heads, grad_ref, y_ref, acc_ref, out_to):
    y_ref[...] = jnp.zeros(y_ref.shape, F32)
    for t in range(types):
        acc = None
        for first in range(0, 12, 2):
            sel = diagonal_select(first)
            for n in range(heads):
                for zq in range(2):
                    for zk in range(2):
                        at = n * 32 + zq * 16 + zk * 8
                        for k in range(2):
                            to = n * TOK + zq * HALF + (first + k) * 6
                            y_ref[at : at + 6, 128 * k : 128 * k + 128] = grad_ref[t, zk, to : to + 6]
            y = y_ref[...]
            hi = low(y)
            part = mm_t(hi, sel) + mm_t(low(y - hi.astype(F32)), sel)
            acc = part if acc is None else acc + part
        for half in range(2):
            acc_ref[half, : heads * 32] = acc[:, 128 * half : 128 * half + 128]
        for g, row in table_groups():
            for half in range(2):
                out_to(t, g * RUN + half * HALF_RUN, acc_ref[half, pl.ds(row, heads, stride=32)][:, :HALF_RUN])


def bias_kernel(fine_ref, next_ref, coarse_ref, fine_out, coarse_out, u_ref):
    at_end = [lax.axis_index(name) == lax.axis_size(name) - 1 for name in ("rep", "lat")]
    own, later, coarse = fine_ref[...], next_ref[...], coarse_ref[...]
    kinds = [
        (own[:, 0, :], False, fine_out.at[0]),
        (own[:, 1, :], True, fine_out.at[1]),
        (later[:, 0, :], False, fine_out.at[2]),
        (coarse[:, 0, :], True, coarse_out.at[0]),
    ]
    expand_tables(at_end, kinds, u_ref)


FIELD_PAD, COT_PAD = 176, 24
MESSAGE = FIELD_PAD + FIELD_PAD // 2 + 3 * COT_PAD


def pack_kernel(field_ref, cot_ref, *outs):
    r = iota((FIELD_PAD, 1), 0)
    row = div_const(r, 18)
    rc = iota((COT_PAD, 1), 0)
    crow = div_const(rc, 6)
    hots, cot_hots = [], []
    for t in range(2):
        for u in range(2):
            target = (row + (0 if t else 3)) * 24 + r - row * 18 + (0 if u else 6)
            hots.append(one_hot(jnp.where(r < 162, target, -1), 288))
    hot = jnp.concatenate(hots, axis=0)
    for s in range(2):
        for t in range(2):
            for u in range(2):
                target = (crow + (0 if t else 3)) * 12 + rc - crow * 6 + (0 if u else 6)
                cot_hots.append(one_hot(jnp.where(rc < 18, target * 2 + 1 - s, -1), TOK))
    cot = mm(jnp.concatenate(cot_hots, axis=0), low(cot_ref[...].astype(F32).reshape(TOK, 384)))
    half = FIELD_PAD // 2
    for s in range(2):
        rows = mm(hot, low(field_ref[1 - s].astype(F32).reshape(288, 192)))
        for n in range(4):
            out = outs[4 * s + n]
            part = rows[n * FIELD_PAD : (n + 1) * FIELD_PAD]
            out[:FIELD_PAD] = low(part[:, :128])
            rest = [low(jnp.concatenate([part[:half, 128:], part[half:, 128:]], axis=1))]
            first = (4 * s + n) * COT_PAD
            rest += [low(cot[first : first + COT_PAD, 128 * c : 128 * c + 128]) for c in range(3)]
            out[FIELD_PAD:] = jnp.concatenate([x.astype(F32) for x in rest], axis=0).astype(BF)


def field_of(ref):
    half = FIELD_PAD // 2
    rest = ref[FIELD_PAD : FIELD_PAD + half].astype(F32)
    rest = jnp.concatenate([rest[:, :64], rest[:, 64:]], axis=0)
    return low(jnp.concatenate([ref[:FIELD_PAD].astype(F32), rest], axis=1))


def cot_of(ref):
    rows = ref[FIELD_PAD:].astype(F32)[FIELD_PAD // 2 :]
    return low(jnp.concatenate([rows[COT_PAD * c : COT_PAD * c + COT_PAD] for c in range(3)], axis=1))


def fine_weights(qkv_ref):
    w = qkv_ref[...]
    return w[:, :192], w[:, 192:384], w[:, 384:]


FINE_TILES = ((0, 128, 4), (128, 64, 2))


def tile_rows(start, slots):
    return slice(start // HEAD * TOK, (start // HEAD + slots) * TOK)


def store_keys(ref, x):
    gap = jnp.zeros((128 - HALF, x.shape[1]), F32)
    for n in range(ref.shape[0]):
        part = x[n * TOK : (n + 1) * TOK]
        for z in range(2):
            ref[n, 128 * z : 128 * z + 128] = low(jnp.concatenate([part[HALF * z : HALF * z + HALF], gap], axis=0))


def main_kernel(
    b000, b001, b010, b011, b100, b101, b110, b111,
    bias_ref, cbias_ref,
    fgain_ref, fqkv_ref, fproj_ref, mgain_ref, mw_ref, cgain_ref, cqkv_ref, cproj_ref,
    x_out, gfo_out, latp_out, lonp_out, cin_out, gy_out, xc_out, mnorm_out, gci_out, mix_ref, g_ref, gb_ref, gains_out,
    x_ref, fo_ref, fq_ref, fk_ref, fv_ref, fm_ref,
    q_ref, k_ref, v_ref, gm_ref,
):
    bufs = ((b000, b001), (b010, b011)), ((b100, b101), (b110, b111))
    _, hh, ww = window_index(HALF)
    seen = set()
    for t in range(2):
        for u in range(2):
            hots = []
            for wr in (t, t + 1):
                for wc in (u, u + 1):
                    lat = 6 * wr + hh - 9 * t
                    lon = 12 * wc + ww - 18 * u
                    good = (lat >= 0) & (lat < 9) & (lon >= 0) & (lon < 18)
                    hots.append(one_hot(jnp.where(good, lat * 18 + lon, -1), FIELD_PAD))
            hot = jnp.concatenate(hots, axis=0)
            for z in range(2):
                part = mm(hot, field_of(bufs[z][t][u]))
                for n in range(4):
                    place = 3 * (t + n // 2) + u + n % 2, slice(z * HALF, (z + 1) * HALF)
                    value = part[n * HALF : (n + 1) * HALF]
                    if (place[0], z) in seen:
                        value = value + x_ref[place]
                    seen.add((place[0], z))
                    x_ref[place] = value
    for wr in range(2):
        for wc in range(2):
            x_out[2 * wr + wc] = low(x_ref[3 * wr + wc])
    wq, wk, wv = fine_weights(fqkv_ref)
    x = x_ref[...].reshape(9 * TOK, 192)
    (hat,), _ = norm([x])
    xn = low(hat * fgain_ref[...].reshape(1, 192))
    fq_ref[...] = low(mm(xn, wq) * HEAD**-0.5).reshape(9, TOK, 192)
    store_keys(fk_ref, mm(xn, wk))
    store_keys(fv_ref, mm(xn, wv))

    def fine_window(w, table_ref, wr):
        for start, width, slots in FINE_TILES:
            lanes = slice(start, start + width)

            bias = load_bias(table_ref, wr, tile_rows(start, slots))
            fm_ref[w, :, lanes] = low(
                tile_forward(fq_ref[w, :, lanes], fk_ref[w, :, lanes], fv_ref[w, :, lanes], bias, slots)
            )

    @pl.loop(0, 9, unroll=3)
    def _(w):
        fine_window(w, bias_ref, div_const(w, 3))

    out = low(mm(fm_ref[...].reshape(9 * TOK, 192), fproj_ref[...])).astype(F32)
    fo_ref[...] = low(x_ref[...].reshape(9 * TOK, 192) + out)

    z, i, j = window_index(TOK)
    hots = []
    for p in range(4):
        lat = 3 + 2 * i + p // 2
        lon = 6 + 2 * j + p % 2
        wr, wc = div_const(lat, 6), div_const(lon, 12)
        target = (3 * wr + wc) * TOK + z * HALF + (lon - 12 * wc) * 6 + lat - 6 * wr
        hots.append(one_hot(target, 9 * TOK))
    merged = mm(jnp.concatenate(hots, axis=0), fo_ref[...])
    merged = [merged[p * TOK : (p + 1) * TOK] for p in range(4)]
    mhat, minv = norm(merged)
    mgain = mgain_ref[...].reshape(1, 768)
    mgain = [mgain[:, 192 * p : 192 * p + 192] for p in range(4)]
    mnorm = [low(h * g) for h, g in zip(mhat, mgain)]
    mweight = [mw_ref[192 * p : 192 * p + 192] for p in range(4)]
    cin = low(sum(mm(n, w) for n, w in zip(mnorm, mweight))).astype(F32)
    (chat,), cinv = norm([cin])
    cgain = cgain_ref[...].reshape(1, 384)
    xc = low(chat * cgain)
    _, ci, cj = window_index(HALF)
    cot_rows = [None, None]
    for t in range(2):
        for u in range(2):
            lat, lon = ci - 3 * t, cj - 6 * u
            good = (lat >= 0) & (lat < 3) & (lon >= 0) & (lon < 6)
            hot = one_hot(jnp.where(good, lat * 6 + lon, -1), COT_PAD)
            for s in range(2):
                part = mm(hot, cot_of(bufs[s][t][u]))
                cot_rows[s] = part if cot_rows[s] is None else cot_rows[s] + part
    cot = jnp.concatenate(cot_rows, axis=0)
    gy = low(cot)
    gmix = low(mm_t(gy, cproj_ref[...]))
    for tile in range(3):
        lanes = slice(128 * tile, 128 * tile + 128)
        q_ref[tile] = low(mm(xc, cqkv_ref[:, lanes]) * HEAD**-0.5)
        k_ref[tile] = pad_keys(mm(xc, cqkv_ref[:, 384 + 128 * tile : 512 + 128 * tile]))
        v_ref[tile] = pad_keys(mm(xc, cqkv_ref[:, 768 + 128 * tile : 896 + 128 * tile]))
        gm_ref[tile] = gmix[:, lanes]

    def coarse_tile(tile, carry):
        rows = pl.ds(pl.multiple_of(tile * 4 * TOK, 64), 4 * TOK)

        def bias_grad_to(gs):
            gb_ref[0, 0, rows] = gs[:, :128]
            gb_ref[0, 1, rows] = gs[:, 128:]

        mixed, gq, gk, gv = tile_both(
            q_ref[tile], k_ref[tile], v_ref[tile], gm_ref[tile], load_bias(cbias_ref, 0, rows), bias_grad_to, 4
        )
        mix_ref[tile] = low(mixed)
        g_ref[0, tile] = low(gq * HEAD**-0.5)
        g_ref[1, tile] = low(unpad_keys(gk))
        g_ref[2, tile] = low(unpad_keys(gv))
        return carry

    lax.fori_loop(0, 3, coarse_tile, 0, unroll=True)
    grolled = None
    for tile in range(3):
        for m in range(3):
            wcols = slice(384 * m + 128 * tile, 384 * m + 128 * tile + 128)
            part = mm_t(g_ref[m, tile], cqkv_ref[:, wcols])
            grolled = part if grolled is None else grolled + part
    cin_out[...] = low(cin)
    gy_out[...] = gy
    xc_out[...] = xc
    (gci,), (cgain_grad,) = norm_back([low(grolled).astype(F32)], [cgain], [chat], cinv)
    gci = low(cot + gci)
    gml = []
    gci_out[...] = gci
    for p in range(4):
        mnorm_out[p] = mnorm[p]
        gml.append(low(mm_t(gci, mweight[p])).astype(F32))
    gmerged, mgain_grad = norm_back(gml, mgain, mhat, minv)
    gains_out[...] = gain_rows(list(mgain_grad) + [cgain_grad])
    r48 = iota((48, 1), 0)
    zi = div_const(r48, 24)
    rest = r48 - 24 * zi
    lat_hot = one_hot(zi * HALF + lax.shift_right_logical(rest, 1) * 6 + 4 + (rest & 1), TOK)
    r40 = iota((40, 1), 0)
    zi = jnp.where(r40 >= 18, 1, 0)
    lon_hot = one_hot(jnp.where(r40 < 36, zi * HALF + 54 + r40 - 18 * zi, -1), TOK)
    hot = jnp.concatenate([lat_hot, lon_hot], axis=0)
    for p in range(4):
        g = low(gmerged[p])
        gfo_out[p] = g
        part = low(mm(hot, g))
        latp_out[48 * p : 48 * p + 48] = part[:48]
        lonp_out[40 * p : 40 * p + 40] = part[48:]


def side_kernel(
    cin_ref, gy_ref, xc_ref, mnorm_ref, gci_ref, mix_ref, g_ref, gb_ref, cproj_ref,
    cout_out, keep_out, send_out, ctab_out, y_ref, acc_ref, pack_out,
):
    gy, xc, gci = gy_ref[...], xc_ref[...], gci_ref[...]
    out = None
    for tile in range(3):
        lanes = slice(128 * tile, 128 * tile + 128)
        part = mm(mix_ref[tile], cproj_ref[lanes])
        out = part if out is None else out + part
        dproj = low(t_mm(mix_ref[tile], gy))
        for c in range(3):
            start = 5760 + 384 * c + 128 * tile
            put(pack_out, COARSE, start, dproj[:, 128 * c : 128 * c + 128])
    cout_out[...] = low(cin_ref[...].astype(F32) + low(out).astype(F32))
    for m in range(3):
        dqkv = low(t_mm(xc, jnp.concatenate([g_ref[m, tile] for tile in range(3)], axis=1)))
        for tile in range(3):
            start = 2304 + 384 * (3 * m + tile)
            put(pack_out, COARSE, start, dqkv[:, 128 * tile : 128 * tile + 128])
    for p in range(4):
        dmw = low(t_mm(mnorm_ref[p], gci))
        for c in range(3):
            start = 768 * c + 192 * p
            put(pack_out, COARSE, start, dmw[:, 128 * c : 128 * c + 128])
    split_halves(pack_out, keep_out, send_out)
    ctab_out[...] = jnp.zeros(ctab_out.shape, F32)

    def ctab(t, start, rows):
        ctab_out[:12, start : start + HALF_RUN] = rows

    fold_tables(1, 12, gb_ref, y_ref, acc_ref, ctab)


QUARTERS = ((0, 0), (0, 1), (1, 1), (1, 0))
FINE_PAD = (176, 64, 32, 64)
PIECE = tuple(n + 48 for n in FINE_PAD)
BASE = tuple(sum(PIECE[:n]) for n in range(5))


def fine_rows_of(s, t, u):
    r = iota((FINE_PAD[QUARTERS.index((t, u))], 1), 0)
    width, height = 6 if u else 18, 3 if t else 9
    row = div_const(r, width)
    lat, lon = row + 9 * t, r - row * width + 18 * u
    wr, wc = div_const(lat, 6), div_const(lon, 12)
    target = (2 * wr + wc) * TOK + s * HALF + (lon - 12 * wc) * 6 + lat - 6 * wr
    return jnp.where(row < height, target, -1)


def coarse_rows_of(s, t, u):
    r = iota((24, 1), 0)
    row = div_const(r, 6)
    return jnp.where(row < 3, s * HALF + (r - row * 6 + 6 * u) * 6 + row + 3 * t, -1)


def back_kernel(
    x_in, gfo_ref, latp_ref, lonp_ref, corner_ref, bias_ref, fgain_ref, fqkv_ref, fproj_ref, ctab_ref, gains_ref, cout_ref,
    near0_out, later0_out, near1_out, later1_out, keep_out, send_out,
    src_ref, fq_ref, fk_ref, fv_ref, fm_ref, gm_ref, g_ref, gb_ref, y_ref, acc_ref, tab_ref, pack_out,
):
    src_ref[:576] = gfo_ref[...]
    src_ref[576:768] = latp_ref[...]
    src_ref[768:928] = lonp_ref[...]
    src_ref[928:] = corner_ref[...]
    z, h, w = window_index(TOK)
    hots = []
    for wr in range(2):
        for wc in range(2):
            lat, lon = 6 * wr + h, 12 * wc + w
            behind, before = lat < 3, lon < 6
            lat = jnp.where(behind, lat + 9, lat - 3)
            lon = jnp.where(before, lon + 18, lon - 6)
            p = 2 * (lat & 1) + (lon & 1)
            i, j = lax.shift_right_logical(lat, 1), lax.shift_right_logical(lon, 1)
            own = p * TOK + z * HALF + j * 6 + i
            from_lat = 576 + p * 48 + z * 24 + j * 2 + i - 4
            from_lon = 768 + p * 40 + z * 18 + (j - 9) * 6 + i
            target = jnp.where(before, from_lon + jnp.where(behind, 160, 0), jnp.where(behind, from_lat, own))
            hots.append(one_hot(target, 1088))
    gy = low(mm(jnp.concatenate(hots, axis=0), src_ref[...]))
    gy32 = gy.astype(F32)
    gb_ref[...] = jnp.zeros(gb_ref.shape, F32)
    weights = fine_weights(fqkv_ref)
    gain = fgain_ref[...].reshape(1, 192)
    x = x_in[...].reshape(4 * TOK, 192).astype(F32)
    (hat,), inv = norm([x])
    xn = low(hat * gain)
    fq_ref[...] = low(mm(xn, weights[0]) * HEAD**-0.5).reshape(4, TOK, 192)
    store_keys(fk_ref, mm(xn, weights[1]))
    store_keys(fv_ref, mm(xn, weights[2]))
    gm_ref[...] = low(mm_t(gy, fproj_ref[...])).reshape(4, TOK, 192)

    @pl.loop(0, 4)
    def _(n):
        wr = lax.shift_right_logical(n, 1)
        for start, width, slots in FINE_TILES:
            lanes = slice(start, start + width)

            rows = tile_rows(start, slots)

            def bias_grad_to(gs):
                gb_ref[wr, 0, rows] += gs[:, :128]
                gb_ref[wr, 1, rows] += gs[:, 128:]

            mixed, gq, gk, gv = tile_both(
                fq_ref[n, :, lanes], fk_ref[n, :, lanes], fv_ref[n, :, lanes], gm_ref[n, :, lanes],
                load_bias(bias_ref, wr, rows), bias_grad_to, slots,
            )
            fm_ref[n, :, lanes] = low(mixed)
            g_ref[0, n, :, lanes] = low(gq * HEAD**-0.5)
            g_ref[1, n, :, lanes] = low(unpad_keys(gk))
            g_ref[2, n, :, lanes] = low(unpad_keys(gv))

    dproj = t_mm(fm_ref[...].reshape(4 * TOK, 192), gy)
    grads = [g_ref[m].reshape(4 * TOK, 192) for m in range(3)]
    dqkv = [t_mm(xn, g) for g in grads]
    grolled = sum(mm_t(g, w) for g, w in zip(grads, weights))
    (gx,), (ggain,) = norm_back([low(grolled).astype(F32)], [gain], [hat], inv)
    fg = low(gy32 + gx)
    cout = cout_ref[...]
    for s, outs in enumerate(((near0_out, later0_out), (near1_out, later1_out))):
        hots, coarse_hots = [], []
        for t, u in QUARTERS:
            hots.append(one_hot(fine_rows_of(s, t, u), 4 * TOK))
            coarse_hots.append(one_hot(coarse_rows_of(s, t, u), TOK))
        fine = low(mm(jnp.concatenate(hots, axis=0), fg))
        coarse = low(mm(jnp.concatenate(coarse_hots, axis=0), cout))
        at = 0
        for n, rows in enumerate(FINE_PAD):
            out, to = outs[n // 2], BASE[n] - BASE[n // 2 * 2]
            out[to : to + rows] = fine[at : at + rows]
            out[to + rows : to + rows + 24] = coarse[24 * n : 24 * n + 24, :192]
            out[to + rows + 24 : to + rows + 48] = coarse[24 * n : 24 * n + 24, 192:]
            at += rows
    first = low(jnp.concatenate([dqkv[0], dqkv[1]], axis=1))
    second = low(jnp.concatenate([dqkv[2], dproj], axis=1))
    for c in range(3):
        put(pack_out, FINE, 192 * c, first[:, 128 * c : 128 * c + 128])
        put(pack_out, FINE, 576 + 192 * c, second[:, 128 * c : 128 * c + 128])
    put(pack_out, FINE, 1152, gain_rows([ggain]))
    put(pack_out, FINE, 1168, gains_ref[...])
    put(pack_out, FINE, 1184, jnp.zeros((96, 128), BF))
    tab_ref[...] = jnp.zeros(tab_ref.shape, F32)
    tab_ref[16:32] = ctab_ref[...]

    def ftab(t, start, rows):
        tab_ref[8 * t : 8 * t + 6, start : start + HALF_RUN] = rows

    fold_tables(2, 6, gb_ref, y_ref, acc_ref, ftab)
    for c in range(13):
        for half in range(2):
            lanes = slice(256 * c + 128 * half, 256 * c + 128 * half + 128)
            pack_out[c, FINE + 32 * half : FINE + 32 * half + 32] = low(tab_ref[:, lanes])
    for c in range(13, 16):
        pack_out[c, FINE:] = jnp.zeros((TAB, 128), BF)
    split_halves(pack_out, keep_out, send_out)


def place_kernel(near0_ref, near1_ref, later0_ref, later1_ref, lon_ref, field_out, coarse_out, src_ref):
    def chosen(later_row, later_col, values):
        value = dict(zip(QUARTERS, values))
        near = jnp.where(later_row, value[1, 0], value[0, 0])
        return jnp.where(later_col, jnp.where(later_row, value[1, 1], value[0, 1]), near)

    base = BASE[:4]
    r = iota((288, 1), 0)
    lat = div_const(r, 24)
    col = r - lat * 24
    later_row, later_col = lat < 3, col < 6
    row = jnp.where(later_row, lat, lat - 3)
    inside = jnp.where(later_col, row * 6 + col, row * 18 + col - 6)
    hots = [one_hot(chosen(later_row, later_col, base) + inside, sum(PIECE))]
    r = iota((HALF, 1), 0)
    lat = div_const(r, 12)
    col = r - lat * 12
    later_row, later_col = lat < 3, col < 6
    inside = jnp.where(later_row, lat, lat - 3) * 6 + jnp.where(later_col, col, col - 6)
    inside = inside + chosen(later_row, later_col, [b + n for b, n in zip(base, FINE_PAD)])
    hots += [one_hot(inside, sum(PIECE)), one_hot(inside + 24, sum(PIECE))]
    hot = jnp.concatenate(hots, axis=0)
    placed = []
    for s in range(2):
        src_ref[: BASE[1]] = (near0_ref, near1_ref)[s][: BASE[1]]
        src_ref[BASE[1] : BASE[3]] = lon_ref[s]
        src_ref[BASE[3] :] = (later0_ref, later1_ref)[s][PIECE[2] :]
        out = low(mm(hot, src_ref[...]))
        for h in range(12):
            field_out[1 - s, h] = out[24 * h : 24 * h + 24]
        coarse = jnp.concatenate([out[288:360], out[360:]], axis=1).astype(F32)
        placed.append(coarse)
    for h in range(6):
        rows = slice(12 * h, 12 * h + 12)
        coarse_out[h] = low(jnp.stack([placed[1][rows], placed[0][rows]], axis=1))


def unpack_kernel(fine_scale, coarse_scale, fine_table_scale, coarse_table_scale, mine_ref, other_ref, *outs):
    sums = mine_ref, other_ref, lax.axis_index("lon") % 2
    fgain_out, qkv_out, proj_out, ftab_out, mgain_out, mw_out, cgain_out, cqkv_out, cproj_out, ctab_out = outs
    def coarse_get(start, count):
        return get(sums, COARSE, 0, start, count) * coarse_scale

    def fine_get(start, count, scale):
        return get(sums, FINE, COARSE, start, count) * scale

    for c in range(3):
        lanes = slice(128 * c, 128 * c + 128)
        mw_out[:, lanes] = coarse_get(768 * c, 768)
        cproj_out[:, lanes] = coarse_get(5760 + 384 * c, 384)
        qkv_out[:, lanes] = fine_get(192 * c, 192, fine_scale)
    for c in range(9):
        cqkv_out[:, 128 * c : 128 * c + 128] = coarse_get(2304 + 384 * c, 384)
    second = [fine_get(576 + 192 * c, 192, fine_scale) for c in range(3)]
    qkv_out[:, 384:512] = second[0]
    qkv_out[:, 512:] = second[1][:, :64]
    proj_out[...] = jnp.concatenate([second[1][:, 64:], second[2]], axis=1)
    gains = fine_get(1168, 16, coarse_scale)
    for c in range(6):
        mgain_out[pl.ds(128 * c, 128)] = gains[c]
    for c in range(3):
        cgain_out[pl.ds(128 * c, 128)] = gains[6 + c]
    gains = fine_get(1152, 16, fine_scale)
    fgain_out[...] = jnp.concatenate([gains[:1], gains[1:2, :64]], axis=1).reshape(192)
    for c in range(13):
        for half in range(2):
            start = 256 * c + 128 * half
            n = min(128, POS - start)
            block = get_chunk(sums, c, slice(GRAIN + 32 * half, GRAIN + 32 * half + 32))[:, :n]
            both = jnp.stack([block[:6], block[8:14]], axis=1)
            ftab_out[:, :, start : start + n] = both * fine_table_scale
            ctab_out[:, 0, start : start + n] = block[16:28] * coarse_table_scale


def call(kernel, out_shapes, scratch=(), smem=0, flops=0, moved=0, vmem=VMEM_LIMIT):
    def run(*args):
        specs = [pl.BlockSpec(memory_space=pltpu.SMEM)] * smem
        specs += [pl.BlockSpec(memory_space=pltpu.VMEM)] * (len(args) - smem)
        return pl.pallas_call(
            kernel,
            out_shape=[jax.ShapeDtypeStruct(s, d) for s, d in out_shapes],
            in_specs=specs,
            out_specs=[pl.BlockSpec(memory_space=pltpu.VMEM)] * len(out_shapes),
            scratch_shapes=[pltpu.VMEM(s, d) for s, d in scratch],
            compiler_params=pltpu.CompilerParams(vmem_limit_bytes=vmem),
            cost_estimate=pl.CostEstimate(flops=flops, bytes_accessed=moved, transcendentals=0),
        )(*args)

    return run


def shifted(x, offset, sign):
    names = [n for n, o in zip(("lon", "lat", "rep"), offset[::-1]) if o]
    sizes = [lax.axis_size(n) for n in names]
    pairs = []
    for place in np.ndindex(*sizes):
        target = [(p - sign) % s for p, s in zip(place, sizes)]
        pairs.append((int(np.ravel_multi_index(place, sizes)), int(np.ravel_multi_index(target, sizes))))
    return lax.ppermute(x, tuple(names), pairs)


CORNERS = [(s, t, u) for s in range(2) for t in range(2) for u in range(2)]


def exchange(x, axes):
    return lax.all_to_all(lax.optimization_barrier(x), axes, 0, 0, tiled=True)


def summed(x):
    return jnp.sum(x.astype(F32), axis=0, keepdims=True).astype(BF)


def spread(x, count):
    return jnp.broadcast_to(x, (count,) + x.shape[1:])


def sibling(x):
    return lax.ppermute(x, "lon", [(i, i ^ 1) for i in range(lax.axis_size("lon"))])


def exchange_columns(x):
    size = lax.axis_size("lon")
    groups = [list(range(core, size, 2)) for core in range(2)]
    return lax.all_to_all(lax.optimization_barrier(x), "lon", 0, 0, axis_index_groups=groups, tiled=True)


def reduce_everywhere(keep, other, near0, later0, near1, later1):
    rest = lax.axis_size("lat") * lax.axis_size("rep")
    keep, other = lax.optimization_barrier((keep, other))
    pair = [(a.astype(F32) + b.astype(F32)).astype(BF) for a, b in zip(keep, other)]
    pack = exchange_columns(jnp.concatenate(pair, axis=1))
    pack = summed(pack)
    part = pack[:, :GRAIN].reshape(rest, -1, 128)
    near1, later0, later1 = (
        shifted(x, place, -1) for x, place in ((near1, (1, 0, 0)), (later0, (0, 1, 0)), (later1, (1, 1, 0)))
    )
    part = exchange(part, ("lat", "rep"))
    part, near1, later0, later1 = lax.optimization_barrier((part, near1, later0, later1))
    part = spread(summed(part), rest)
    column = [jnp.concatenate([x[BASE[1] :], y[: PIECE[2]]]) for x, y in ((near0, later0), (near1, later1))]
    column = shifted(jnp.stack(column), (0, 0, 1), -1)
    part, column = lax.optimization_barrier((exchange(part, ("lat", "rep")), column))
    mine = jnp.concatenate([part.reshape(1, GRAIN, 128), pack[:, GRAIN:]], axis=1)
    mine = exchange_columns(spread(mine, lax.axis_size("lon") // 2))
    return (mine, sibling(mine)), (near0, near1, later0, later1, column)


def body(
    fine_field, fine_gain, fine_qkv, fine_proj, fine_table, merge_gain, merge_weight,
    coarse_gain, coarse_qkv, coarse_proj, coarse_table, cotangent,
):
    rep, lat, lon = (lax.axis_size(n) for n in ("rep", "lat", "lon"))
    packs = call(pack_kernel, [((MESSAGE, 128), BF)] * 8)(fine_field, cotangent.transpose(1, 2, 0, 3))
    bufs = [shifted(b, place, 1) if any(place) else b for b, place in zip(packs, CORNERS)]
    table = fine_table[0].transpose(1, 0, 2)
    bias, cbias = call(
        bias_kernel,
        [((3, 2, FINE_ROWS, 128), F32), ((1, 2, COARSE_ROWS, 128), F32)],
        [((2, 34 * 32, 128), F32)],
        flops=1 << 32,
    )(table, shifted(fine_table, (0, 1, 0), 1)[0].transpose(1, 0, 2), coarse_table[0].transpose(1, 0, 2))
    x, gfo, latp, lonp, *coarse, cgains = call(
        main_kernel,
        [
            ((4, TOK, 192), BF), ((4, TOK, 192), BF), ((192, 192), BF), ((160, 192), BF),
            ((TOK, 384), BF), ((TOK, 384), BF), ((TOK, 384), BF), ((4, TOK, 192), BF), ((TOK, 384), BF),
            ((3, TOK, 128), BF), ((3, 3, TOK, 128), BF), ((1, 2, COARSE_ROWS, 128), F32), ((16, 128), BF),
        ],
        [
            ((9, TOK, 192), F32), ((9 * TOK, 192), BF),
            ((9, TOK, 192), BF), ((9, LANES, 192), BF), ((9, LANES, 192), BF), ((9, TOK, 192), BF),
            ((3, TOK, 128), BF), ((3, LANES, 128), BF), ((3, LANES, 128), BF), ((3, TOK, 128), BF),
        ],
        flops=1 << 34,
    )(
        *bufs, bias, cbias, fine_gain, fine_qkv, fine_proj, merge_gain,
        merge_weight, coarse_gain, coarse_qkv, coarse_proj,
    )
    lat_recv = shifted(latp, (0, 1, 0), -1)
    lon_recv = shifted(lonp, (0, 0, 1), -1)
    corner_recv = shifted(lonp, (0, 1, 1), -1)
    cout, ckeep, csend, ctab = call(
        side_kernel,
        [((TOK, 384), BF), ((8, COARSE, 128), BF), ((8, COARSE, 128), BF), ((16, WIDE), F32)],
        [((384, 256), F32), ((2, 512, 128), F32), ((16, COARSE, 128), BF)],
        flops=1 << 35,
    )(*coarse, coarse_proj)
    cother = sibling(csend)
    near0, later0, near1, later1, fkeep, fsend = call(
        back_kernel,
        [((BASE[2], 192), BF), ((BASE[4] - BASE[2], 192), BF),
         ((BASE[2], 192), BF), ((BASE[4] - BASE[2], 192), BF), ((8, FINE + TAB, 128), BF), ((8, FINE + TAB, 128), BF)],
        [
            ((1088, 192), BF), ((4, TOK, 192), BF), ((4, LANES, 192), BF), ((4, LANES, 192), BF),
            ((4, TOK, 192), BF), ((4, TOK, 192), BF), ((3, 4, TOK, 192), BF),
            ((2, 2, FINE_ROWS, 128), F32), ((192, 256), F32), ((2, 256, 128), F32), ((32, WIDE), F32), ((16, FINE + TAB, 128), BF),
        ],
        flops=1 << 33,
    )(x, gfo.reshape(4 * TOK, 192), lat_recv, lon_recv, corner_recv, bias, fine_gain, fine_qkv, fine_proj, ctab, cgains, cout)
    sums, back = reduce_everywhere((ckeep, fkeep), (cother, sibling(fsend)), near0, later0, near1, later1)
    field_grad, coarse_out = call(
        place_kernel, [((2, 12, 24, 192), BF), ((6, 12, 2, 384), BF)], [((sum(PIECE), 192), BF)]
    )(*back)
    levels, rows, cols = 2 * rep, 12 * lat, 24 * lon
    fine_scale = (levels * rows * cols) ** -0.5
    coarse_scale = (levels * rows * cols // 4) ** -0.5
    fine_table_scale = (cols // 12) ** -0.5
    coarse_table_scale = (cols // 24) ** -0.5
    fgain_g, fqkv_g, fproj_g, ftab_g, mgain_g, mw_g, cgain_g, cqkv_g, cproj_g, ctab_g = call(
        lambda *refs: unpack_kernel(fine_scale, coarse_scale, fine_table_scale, coarse_table_scale, *refs),
        [
            ((192,), F32), ((192, 576), F32), ((192, 192), F32), ((6, 2, POS), F32), ((768,), F32),
            ((768, 384), F32), ((384,), F32), ((384, 1152), F32), ((384, 384), F32), ((12, 1, POS), F32),
        ],
    )(*sums)
    return (
        coarse_out.transpose(2, 0, 1, 3), field_grad, fgain_g, fqkv_g, fproj_g, ftab_g.transpose(1, 0, 2)[None],
        mgain_g, mw_g, cgain_g, cqkv_g, cproj_g, ctab_g.transpose(1, 0, 2)[None],
    )


def solution(mesh):
    tokens, tables = P("rep", "lat", "lon", None), P("rep", "lat", None, None)
    return jax.shard_map(
        body,
        mesh=mesh,
        in_specs=(tokens, P(), P(), P(), tables, P(), P(), P(), P(), P(), tables, tokens),
        out_specs=(tokens, tokens, P(), P(), P(), tables, P(), P(), P(), P(), P(), tables),
        check_vma=False,
    )
```

profile of v0, /device:TPU:1, one launch (start us, length us, event | category | flops | bytes accessed | tf_op | source)
XLA Modules:
  0.0 141.4 jit_solution(10709889866158028470)
XLA Ops:
  0.6 6.5 %collective-permute-start.7 = (f32[1,2,6,3312]{3,1,2,0:T(2,128)}, f32[1,2,6,3312]{3,1,2,0:T(2,128)S(1)}, u32[]{:S(2)}, u32[]{:S(2)}) collective-permute-start(f32[1,2,6,3312]{3,1,2,0:T(2,128)} %param.16), channel_id=1, source_target_pairs={{0,14},{2,0},{4,2},{6,4},{8,6},{10,8},{12,10},{14,12},{1,15},{3,1}... | collective-permute-start | bytes 476936 | tf_op jit(solution)/shard_map/ppermute | solution.py:758
  11.4 5.5 %collective-permute-start.2 = (bf16[336,128]{1,0:T(8,128)(2,1)S(1)}, bf16[336,128]{1,0:T(8,128)(2,1)S(1)}, u32[]{:S(2)}, u32[]{:S(2)}) collective-permute-start(bf16[336,128]{1,0:T(8,128)(2,1)S(1)} %get-tuple-element.70), channel_id=1, source_target_pairs={{0,254},{2,240},{4,242},{6,244},{8,246},{10,248},{12,250},{14,252}... | collective-permute-start | bytes 258056 | tf_op jit(solution)/shard_map/ppermute | solution.py:758
  17.3 1.8 %collective-permute-start.4 = (bf16[336,128]{1,0:T(8,128)(2,1)S(1)}, bf16[336,128]{1,0:T(8,128)(2,1)S(1)}, u32[]{:S(2)}, u32[]{:S(2)}) collective-permute-start(bf16[336,128]{1,0:T(8,128)(2,1)S(1)} %get-tuple-element.72), channel_id=1, source_target_pairs={{0,241},{1,240},{16,1},{17,0},{32,17},{33,16},{48,33},{49,32},{64,... | collective-permute-start | bytes 258056 | tf_op jit(solution)/shard_map/ppermute | solution.py:758
  19.9 5.2 %collective-permute-start.6 = (bf16[336,128]{1,0:T(8,128)(2,1)S(1)}, bf16[336,128]{1,0:T(8,128)(2,1)S(1)}, u32[]{:S(2)}, u32[]{:S(2)}) collective-permute-start(bf16[336,128]{1,0:T(8,128)(2,1)S(1)} %get-tuple-element.74), channel_id=1, source_target_pairs={{0,255},{1,254},{2,241},{3,240},{4,243},{5,242},{6,245},{7,244},{8... | collective-permute-start | bytes 258056 | tf_op jit(solution)/shard_map/ppermute | solution.py:758
  27.0 3.3 %shard_map.212 = (f32[3,2,872,128]{3,2,1,0:T(8,128)S(1)}, f32[1,2,1736,128]{3,2,1,0:T(8,128)S(1)}) custom-call(f32[6,2,3312]{2,1,0:T(2,128)S(1)} %bitcast.26, f32[6,2,3312]{2,1,0:T(2,128)S(1)} %bitcast.28, f32[12,1,3312]{2,1,0:T(1,128)S(1)} %bitcast.27), custom_call_target="tpu_custom_call" | custom-call | flops 4294967296 | tf_op jit(solution)/shard_map/pallas_call | solution.py:738
  30.4 11.2 %shard_map.213 = (bf16[4,144,192]{2,1,0:T(8,128)(2,1)S(1)}, bf16[4,144,192]{2,1,0:T(8,128)(2,1)S(1)}, bf16[192,192]{1,0:T(8,128)(2,1)S(1)}, bf16[160,192]{1,0:T(...) custom-call(bf16[336,128]{1,0:T(8,128)(2,1)S(1)} %get-tuple-element., ...), custom_call_target="tpu_custom_call" | custom-call | flops 17179869184 | tf_op jit(solution)/shard_map/pallas_call | solution.py:738
  42.8 2.9 %shard_map.214 = (bf16[144,384]{1,0:T(8,128)(2,1)S(1)}, bf16[8,432,128]{2,1,0:T(8,128)(2,1)S(1)}, bf16[8,432,128]{2,1,0:T(8,128)(2,1)S(1)}, f32[16,3456]{1,0:T(8,128)S(1)}) custom-call(bf16[144,384]{1,0:T(8,128)(2,1)S(1)} %get-tuple-element.81.cin_ref, bf16[144,384]{1,0:T(8,128)(2,1)S(1)} %get-tuple-element.82.gy_ref, ...), custom_call_target="tpu_custom_call" | custom-call | flops 34359738368 | tf_op jit(solution)/shard_map/pallas_call | solution.py:738
  47.9 10.4 %shard_map.215 = (bf16[336,192]{1,0:T(8,128)(2,1)S(1)}, bf16[192,192]{1,0:T(8,128)(2,1)S(1)}, bf16[336,192]{1,0:T(8,128)(2,1)S(1)}, bf16[192,192]{1,0:T(8,128)(2...) custom-call(bf16[4,144,192]{2,1,0:T(8,128)(2,1)S(1)} %get-tuple-element.77.x_in, ...), custom_call_target="tpu_custom_call" | custom-call | flops 8589934592 | tf_op jit(solution)/shard_map/pallas_call | solution.py:738
  58.3 3.2 %collective-permute-start.12 = (bf16[8,144,128]{2,1,0:T(8,128)(2,1)S(1)}, bf16[8,144,128]{2,1,0:T(8,128)(2,1)S(1)}, u32[]{:S(2)}, u32[]{:S(2)}) collective-permute-start(bf16[8,144,128]{2,1,0:T(8,128)(2,1)S(1)} %get-tuple-element.96), channel_id=1, source_target_pairs={{0,16},{16,0},{32,48},{48,32},{64,80},{80,64},{96,112},{112,96},{1... | collective-permute-start | bytes 884744 | tf_op jit(solution)/shard_map/ppermute | solution.py:777
  61.5 1.2 collective-permute-done.12
  63.2 21.0 %all_to_all.20 = bf16[8,576,128]{2,1,0:T(8,128)(2,1)S(1)} all-to-all(bf16[8,576,128]{2,1,0:T(8,128)(2,1)S(1)} %pad_maximum_fusion), channel_id=1, replica_groups={{0,32,64,96,128,160,192,224},{16,48,80,112,144,176,208,240},{1,33,65,97..., dimensions={0} | all-to-all | bytes 2359296 | tf_op jit(solution)/shard_map/all_to_all | solution.py:783
  85.0 3.5 %all-to-all-start.1 = ((bf16[16,32,128]{2,1,0:T(8,128)(2,1)}), bf16[16,32,128]{2,1,0:T(8,128)(2,1)S(1)}, u32[]{:S(2)}, u32[]{:S(2)}) async-start(bf16[16,32,128]{2,1,0:T(8,128)(2,1)} %bitcast.8), calls=%async_computation.1 | async-start | bytes 262144 | tf_op jit(solution)/shard_map/all_to_all | solution.py:765
  88.6 1.2 collective-permute-start.13
  89.8 1.2 collective-permute-start.14
  92.2 3.3 %collective-permute-done.14.later0_ref = bf16[192,192]{1,0:T(8,128)(2,1)S(1)} collective-permute-done((bf16[192,192]{1,0:T(8,128)(2,1)S(1)}, bf16[192,192]{1,0:T(8,128)(2,1)S(1)}, u32[]{:S(2)}, u32[]{:S(2)}) %collective-permute-start.14) | collective-permute-done | bytes 73760 | tf_op jit(solution)/shard_map/ppermute | solution.py:758
  95.5 3.2 %collective-permute-done.15.later1_ref = bf16[192,192]{1,0:T(8,128)(2,1)S(1)} collective-permute-done((bf16[192,192]{1,0:T(8,128)(2,1)S(1)}, bf16[192,192]{1,0:T(8,128)(2,1)S(1)}, u32[]{:S(2)}, u32[]{:S(2)}) %collective-permute-start.15) | collective-permute-done | bytes 73760 | tf_op jit(solution)/shard_map/ppermute | solution.py:758
  99.5 5.1 %all-to-all-start.2 = ((bf16[16,32,128]{2,1,0:T(8,128)(2,1)}), bf16[16,32,128]{2,1,0:T(8,128)(2,1)S(1)}, u32[]{:S(2)}, u32[]{:S(2)}) async-start(bf16[16,32,128]{2,1,0:T(8,128)(2,1)} %broadcast_in_dim.8), calls=%async_computation.2 | async-start | bytes 262144 | tf_op jit(solution)/shard_map/all_to_all | solution.py:765
  104.6 3.3 %collective-permute-start.16 = (bf16[2,192,192]{2,1,0:T(8,128)(2,1)S(1)}, bf16[2,192,192]{2,1,0:T(8,128)(2,1)S(1)}, u32[]{:S(2)}, u32[]{:S(2)}) collective-permute-start(bf16[2,192,192]{2,1,0:T(8,128)(2,1)S(1)} %pad_maximum_fusion.1), channel_id=1, source_target_pairs={{0,16},{16,32},{32,48},{48,64},{64,80},{80,96},{96,112},{112,128},... | collective-permute-start | bytes 442376 | tf_op jit(solution)/shard_map/ppermute | solution.py:758
  107.9 2.6 %collective-permute-done.16.lon_ref = bf16[2,192,192]{2,1,0:T(8,128)(2,1)S(1)} collective-permute-done((bf16[2,192,192]{2,1,0:T(8,128)(2,1)S(1)}, bf16[2,192,192]{2,1,0:T(8,128)(2,1)S(1)}, u32[]{:S(2)}, u32[]{:S(2)}) %collective-permute-start.16) | collective-permute-done | bytes 147488 | tf_op jit(solution)/shard_map/ppermute | solution.py:758
  110.5 2.6 %all-to-all-done.2 = bf16[16,32,128]{2,1,0:T(8,128)(2,1)S(1)} async-done(((bf16[16,32,128]{2,1,0:T(8,128)(2,1)}), bf16[16,32,128]{2,1,0:T(8,128)(2,1)S(1)}, u32[]{:S(2)}, u32[]{:S(2)}) %all-to-all-start.2) | async-done | bytes 131104 | tf_op jit(solution)/shard_map/all_to_all | solution.py:765
  113.4 18.3 %all_to_all.21.refs_0_ = bf16[8,576,128]{2,1,0:T(8,128)(2,1)S(1)} all-to-all(bf16[8,576,128]{2,1,0:T(8,128)(2,1)S(1)} %broadcast_in_dim.19), channel_id=1, replica_groups={{0,32,64,96,128,160,192,224},{16,48,80,112,144,176,208,240},{1,33,65,97..., dimensions={0} | all-to-all | bytes 2359296 | tf_op jit(solution)/shard_map/all_to_all | solution.py:783
  131.7 4.9 %collective-permute-start.17 = (bf16[8,576,128]{2,1,0:T(8,128)(2,1)S(1)}, bf16[8,576,128]{2,1,0:T(8,128)(2,1)S(1)}, u32[]{:S(2)}, u32[]{:S(2)}) collective-permute-start(bf16[8,576,128]{2,1,0:T(8,128)(2,1)S(1)} %all_to_all.21.refs_0_), channel_id=1, source_target_pairs={{0,16},{16,0},{32,48},{48,32},{64,80},{80,64},{96,112},{112,96},{1... | collective-permute-start | bytes 3538952 | tf_op jit(solution)/shard_map/ppermute | solution.py:777
  136.6 1.5 %shard_map.216 = (bf16[2,12,24,192]{3,2,1,0:T(8,128)(2,1)}, bf16[6,12,2,384]{3,2,1,0:T(2,128)(2,1)}) custom-call(bf16[336,192]{1,0:T(8,128)(2,1)S(1)} %get-tuple-element.92.near0_ref, bf16[336,192]{1,0:T(8,128)(2,1)S(1)} %collective-permute-done.13.near1_ref, bf16[192,192]{1,0:T(8,128)(2,1)S(1)} %collective-permute-done.14.later0_ref, ...), custom_call_target="tpu_custom_call" | custom-call | tf_op jit(solution)/shard_map/pallas_call | solution.py:738
  139.0 2.4 %shard_map.217 = (f32[192]{0:T(256)}, f32[192,576]{1,0:T(8,128)}, f32[192,192]{1,0:T(8,128)}, f32[6,2,3312]{2,1,0:T(2,128)}, f32[768]{0:T(1024)}, /*index=5*/f32...) custom-call(bf16[8,576,128]{2,1,0:T(8,128)(2,1)S(1)} %all_to_all.21.refs_0_, ...), custom_call_target="tpu_custom_call" | custom-call | tf_op jit(solution)/shard_map/pallas_call | solution.py:738
  (65 shorter events, 15.1 us)
Async XLA Ops:
  0.6 19.2 %collective-permute-start.7 = (f32[1,2,6,3312]{3,1,2,0:T(2,128)}, f32[1,2,6,3312]{3,1,2,0:T(2,128)S(1)}, u32[]{:S(2)}, u32[]{:S(2)}) collective-permute-start(f32[1,2,6,3312]{3,1,2,0:T(2,128)} %param.16), channel_id=1, source_target_pairs={{0,14},{2,0},{4,2},{6,4},{8,6},{10,8},{12,10},{14,12},{1,15},{3,1}... | collective-permute-start | bytes 476936 | tf_op jit(solution)/shard_map/ppermute | solution.py:758
  9.7 7.6 %collective-permute-start = (bf16[336,128]{1,0:T(8,128)(2,1)S(1)}, bf16[336,128]{1,0:T(8,128)(2,1)S(1)}, u32[]{:S(2)}, u32[]{:S(2)}) collective-permute-start(bf16[336,128]{1,0:T(8,128)(2,1)S(1)} %get-tuple-element.68), channel_id=1, source_target_pairs={{0,240},{16,0},{32,16},{48,32},{64,48},{80,64},{96,80},{112,96},{1... | collective-permute-start | bytes 258056 | tf_op jit(solution)/shard_map/ppermute | solution.py:758
  10.7 8.4 %collective-permute-start.1 = (bf16[336,128]{1,0:T(8,128)(2,1)S(1)}, bf16[336,128]{1,0:T(8,128)(2,1)S(1)}, u32[]{:S(2)}, u32[]{:S(2)}) collective-permute-start(bf16[336,128]{1,0:T(8,128)(2,1)S(1)} %get-tuple-element.69), channel_id=1, source_target_pairs={{0,14},{2,0},{4,2},{6,4},{8,6},{10,8},{12,10},{14,12},{1,15},{3,1}... | collective-permute-start | bytes 258056 | tf_op jit(solution)/shard_map/ppermute | solution.py:758
  11.4 18.9 %collective-permute-start.2 = (bf16[336,128]{1,0:T(8,128)(2,1)S(1)}, bf16[336,128]{1,0:T(8,128)(2,1)S(1)}, u32[]{:S(2)}, u32[]{:S(2)}) collective-permute-start(bf16[336,128]{1,0:T(8,128)(2,1)S(1)} %get-tuple-element.70), channel_id=1, source_target_pairs={{0,254},{2,240},{4,242},{6,244},{8,246},{10,248},{12,250},{14,252}... | collective-permute-start | bytes 258056 | tf_op jit(solution)/shard_map/ppermute | solution.py:758
  17.0 13.3 %collective-permute-start.3 = (bf16[336,128]{1,0:T(8,128)(2,1)S(1)}, bf16[336,128]{1,0:T(8,128)(2,1)S(1)}, u32[]{:S(2)}, u32[]{:S(2)}) collective-permute-start(bf16[336,128]{1,0:T(8,128)(2,1)S(1)} %get-tuple-element.71), channel_id=1, source_target_pairs={{0,1},{1,0},{2,3},{3,2},{4,5},{5,4},{6,7},{7,6},{8,9},{9,8},{10,11... | collective-permute-start | bytes 258056 | tf_op jit(solution)/shard_map/ppermute | solution.py:758
  17.3 13.0 %collective-permute-start.4 = (bf16[336,128]{1,0:T(8,128)(2,1)S(1)}, bf16[336,128]{1,0:T(8,128)(2,1)S(1)}, u32[]{:S(2)}, u32[]{:S(2)}) collective-permute-start(bf16[336,128]{1,0:T(8,128)(2,1)S(1)} %get-tuple-element.72), channel_id=1, source_target_pairs={{0,241},{1,240},{16,1},{17,0},{32,17},{33,16},{48,33},{49,32},{64,... | collective-permute-start | bytes 258056 | tf_op jit(solution)/shard_map/ppermute | solution.py:758
  19.1 11.2 %collective-permute-start.5 = (bf16[336,128]{1,0:T(8,128)(2,1)S(1)}, bf16[336,128]{1,0:T(8,128)(2,1)S(1)}, u32[]{:S(2)}, u32[]{:S(2)}) collective-permute-start(bf16[336,128]{1,0:T(8,128)(2,1)S(1)} %get-tuple-element.73), channel_id=1, source_target_pairs={{0,15},{1,14},{2,1},{3,0},{4,3},{5,2},{6,5},{7,4},{8,7},{9,6},{10,... | collective-permute-start | bytes 258056 | tf_op jit(solution)/shard_map/ppermute | solution.py:758
  19.9 10.5 %collective-permute-start.6 = (bf16[336,128]{1,0:T(8,128)(2,1)S(1)}, bf16[336,128]{1,0:T(8,128)(2,1)S(1)}, u32[]{:S(2)}, u32[]{:S(2)}) collective-permute-start(bf16[336,128]{1,0:T(8,128)(2,1)S(1)} %get-tuple-element.74), channel_id=1, source_target_pairs={{0,255},{1,254},{2,241},{3,240},{4,243},{5,242},{6,245},{7,244},{8... | collective-permute-start | bytes 258056 | tf_op jit(solution)/shard_map/ppermute | solution.py:758
  27.0 3.4 %copy-start.5 = (bf16[192,576]{1,0:T(8,128)(2,1)S(1)}, bf16[192,576]{1,0:T(8,128)(2,1)}, u32[]{:S(2)}) copy-start(bf16[192,576]{1,0:T(8,128)(2,1)} %fqkv_ref.3) | copy-start | bytes 663556
  27.0 3.4 %copy-start.8 = (bf16[192,192]{1,0:T(8,128)(2,1)S(1)}, bf16[192,192]{1,0:T(8,128)(2,1)}, u32[]{:S(2)}) copy-start(bf16[192,192]{1,0:T(8,128)(2,1)} %fproj_ref.3) | copy-start | bytes 221188
  27.0 3.4 %copy-start.9 = (f32[768]{0:T(1024)S(1)}, f32[768]{0:T(1024)}, u32[]{:S(2)}) copy-start(f32[768]{0:T(1024)} %mgain_ref.1) | copy-start | bytes 9220
  27.0 3.4 %copy-start.10 = (f32[384]{0:T(512)S(1)}, f32[384]{0:T(512)}, u32[]{:S(2)}) copy-start(f32[384]{0:T(512)} %cgain_ref.1) | copy-start | bytes 4612
  41.6 6.3 %collective-permute-start.10 = (bf16[160,192]{1,0:T(8,128)(2,1)S(1)}, bf16[160,192]{1,0:T(8,128)(2,1)S(1)}, u32[]{:S(2)}, u32[]{:S(2)}) collective-permute-start(bf16[160,192]{1,0:T(8,128)(2,1)S(1)} %get-tuple-element.80), channel_id=1, source_target_pairs={{0,18},{2,20},{4,22},{6,24},{8,26},{10,28},{12,30},{14,16},{16,34}... | collective-permute-start | bytes 184328 | tf_op jit(solution)/shard_map/ppermute | solution.py:758
  41.7 6.2 %collective-permute-start.9 = (bf16[160,192]{1,0:T(8,128)(2,1)S(1)}, bf16[160,192]{1,0:T(8,128)(2,1)S(1)}, u32[]{:S(2)}, u32[]{:S(2)}) collective-permute-start(bf16[160,192]{1,0:T(8,128)(2,1)S(1)} %get-tuple-element.80), channel_id=1, source_target_pairs={{0,16},{16,32},{32,48},{48,64},{64,80},{80,96},{96,112},{112,128},... | collective-permute-start | bytes 184328 | tf_op jit(solution)/shard_map/ppermute | solution.py:758
  41.8 6.1 %collective-permute-start.8 = (bf16[192,192]{1,0:T(8,128)(2,1)S(1)}, bf16[192,192]{1,0:T(8,128)(2,1)S(1)}, u32[]{:S(2)}, u32[]{:S(2)}) collective-permute-start(bf16[192,192]{1,0:T(8,128)(2,1)S(1)} %get-tuple-element.79), channel_id=1, source_target_pairs={{0,2},{2,4},{4,6},{6,8},{8,10},{10,12},{12,14},{14,0},{1,3},{3,5},... | collective-permute-start | bytes 221192 | tf_op jit(solution)/shard_map/ppermute | solution.py:758
  45.7 17.1 %collective-permute-start.11 = (bf16[8,432,128]{2,1,0:T(8,128)(2,1)S(1)}, bf16[8,432,128]{2,1,0:T(8,128)(2,1)S(1)}, u32[]{:S(2)}, u32[]{:S(2)}) collective-permute-start(bf16[8,432,128]{2,1,0:T(8,128)(2,1)S(1)} %get-tuple-element.95), channel_id=1, source_target_pairs={{0,16},{16,0},{32,48},{48,32},{64,80},{80,64},{96,112},{112,96},{1... | collective-permute-start | bytes 2654216 | tf_op jit(solution)/shard_map/ppermute | solution.py:777
  58.3 4.4 %collective-permute-start.12 = (bf16[8,144,128]{2,1,0:T(8,128)(2,1)S(1)}, bf16[8,144,128]{2,1,0:T(8,128)(2,1)S(1)}, u32[]{:S(2)}, u32[]{:S(2)}) collective-permute-start(bf16[8,144,128]{2,1,0:T(8,128)(2,1)S(1)} %get-tuple-element.96), channel_id=1, source_target_pairs={{0,16},{16,0},{32,48},{48,32},{64,80},{80,64},{96,112},{112,96},{1... | collective-permute-start | bytes 884744 | tf_op jit(solution)/shard_map/ppermute | solution.py:777
  85.0 13.7 %all-to-all-start.1 = ((bf16[16,32,128]{2,1,0:T(8,128)(2,1)}), bf16[16,32,128]{2,1,0:T(8,128)(2,1)S(1)}, u32[]{:S(2)}, u32[]{:S(2)}) async-start(bf16[16,32,128]{2,1,0:T(8,128)(2,1)} %bitcast.8), calls=%async_computation.1 | async-start | bytes 262144 | tf_op jit(solution)/shard_map/all_to_all | solution.py:765
  88.6 10.2 %collective-permute-start.13 = (bf16[336,192]{1,0:T(8,128)(2,1)S(1)}, bf16[336,192]{1,0:T(8,128)(2,1)S(1)}, u32[]{:S(2)}, u32[]{:S(2)}) collective-permute-start(bf16[336,192]{1,0:T(8,128)(2,1)S(1)} %get-tuple-element.101), channel_id=1, source_target_pairs={{0,1},{1,0},{2,3},{3,2},{4,5},{5,4},{6,7},{7,6},{8,9},{9,8},{10,11... | collective-permute-start | bytes 387080 | tf_op jit(solution)/shard_map/ppermute | solution.py:758
  89.8 5.7 %collective-permute-start.14 = (bf16[192,192]{1,0:T(8,128)(2,1)S(1)}, bf16[192,192]{1,0:T(8,128)(2,1)S(1)}, u32[]{:S(2)}, u32[]{:S(2)}) collective-permute-start(bf16[192,192]{1,0:T(8,128)(2,1)S(1)} %get-tuple-element.102), channel_id=1, source_target_pairs={{0,2},{2,4},{4,6},{6,8},{8,10},{10,12},{12,14},{14,0},{1,3},{3,5},... | collective-permute-start | bytes 221192 | tf_op jit(solution)/shard_map/ppermute | solution.py:758
  91.0 7.7 %collective-permute-start.15 = (bf16[192,192]{1,0:T(8,128)(2,1)S(1)}, bf16[192,192]{1,0:T(8,128)(2,1)S(1)}, u32[]{:S(2)}, u32[]{:S(2)}) collective-permute-start(bf16[192,192]{1,0:T(8,128)(2,1)S(1)} %get-tuple-element.103), channel_id=1, source_target_pairs={{0,3},{1,2},{2,5},{3,4},{4,7},{5,6},{6,9},{7,8},{8,11},{9,10},{10,... | collective-permute-start | bytes 221192 | tf_op jit(solution)/shard_map/ppermute | solution.py:758
  99.5 13.7 %all-to-all-start.2 = ((bf16[16,32,128]{2,1,0:T(8,128)(2,1)}), bf16[16,32,128]{2,1,0:T(8,128)(2,1)S(1)}, u32[]{:S(2)}, u32[]{:S(2)}) async-start(bf16[16,32,128]{2,1,0:T(8,128)(2,1)} %broadcast_in_dim.8), calls=%async_computation.2 | async-start | bytes 262144 | tf_op jit(solution)/shard_map/all_to_all | solution.py:765
  104.6 5.9 %collective-permute-start.16 = (bf16[2,192,192]{2,1,0:T(8,128)(2,1)S(1)}, bf16[2,192,192]{2,1,0:T(8,128)(2,1)S(1)}, u32[]{:S(2)}, u32[]{:S(2)}) collective-permute-start(bf16[2,192,192]{2,1,0:T(8,128)(2,1)S(1)} %pad_maximum_fusion.1), channel_id=1, source_target_pairs={{0,16},{16,32},{32,48},{48,64},{64,80},{80,96},{96,112},{112,128},... | collective-permute-start | bytes 442376 | tf_op jit(solution)/shard_map/ppermute | solution.py:758
  131.7 7.3 %collective-permute-start.17 = (bf16[8,576,128]{2,1,0:T(8,128)(2,1)S(1)}, bf16[8,576,128]{2,1,0:T(8,128)(2,1)S(1)}, u32[]{:S(2)}, u32[]{:S(2)}) collective-permute-start(bf16[8,576,128]{2,1,0:T(8,128)(2,1)S(1)} %all_to_all.21.refs_0_), channel_id=1, source_target_pairs={{0,16},{16,0},{32,48},{48,32},{64,80},{80,64},{96,112},{112,96},{1... | collective-permute-start | bytes 3538952 | tf_op jit(solution)/shard_map/ppermute | solution.py:777
  (8 other events, 17.3 us)
where the time goes:
time: 142 us; the launch traced here: 141 us
  starting transfers between devices  47.8 us (34%)
  blocking collectives  39.4 us (28%)
  Pallas kernels  32.2 us (23%)
  waiting for transfers between devices  15.2 us (11%)
  local copies, waits for them, and re-layouts  5.24 us (4%)
    all_to_all x2, blocking collectives, exchange_columns(): lax.all_to_all(lax.optimization_barrier(x), 'lon', 0, 0, axis_index_group...  39.4 us
    pallas_call x7, Pallas kernels, run(): pl.pallas_call(kernel, out_shape=[jax.ShapeDtypeStruct(s, d) for s, d in...  32.2 us
    ppermute x15, starting transfers between devices, shifted(): return lax.ppermute(x, tuple(names), pairs)  30 us
    ppermute x15, waiting for transfers between devices, shifted(): return lax.ppermute(x, tuple(names), pairs)  10.3 us
    ppermute x3, starting transfers between devices, sibling(): lax.ppermute(x, 'lon', [(i, i ^ 1) for i in range(lax.axis_size('lon'))])  9.13 us
    all_to_all x2, starting transfers between devices, exchange(): return lax.all_to_all(lax.optimization_barrier(x), axes, 0, 0, tiled=True)  8.58 us
    unnamed x24, local copies, waits for them, and re-layouts  3.72 us
  transfers between devices with their start and end apart: 20, of which 7 were waited for; matrix products, arithmetic and copies ran while one was open for 0% of the time, Pallas kernels for 13%

commit v1 on v0

--- a/solution.py
+++ b/solution.py
@@ -788,8 +788,8 @@
     keep, other = lax.optimization_barrier((keep, other))
     pair = [(a.astype(F32) + b.astype(F32)).astype(BF) for a, b in zip(keep, other)]
     pack = exchange_columns(jnp.concatenate(pair, axis=1))
-    pack = summed(pack)
-    part = pack[:, :GRAIN].reshape(rest, -1, 128)
+    part = summed(pack[:, :GRAIN]).reshape(rest, -1, 128)
+    tables = summed(pack[:, GRAIN:])
     near1, later0, later1 = (
         shifted(x, place, -1) for x, place in ((near1, (1, 0, 0)), (later0, (0, 1, 0)), (later1, (1, 1, 0)))
     )
@@ -799,7 +799,7 @@
     column = [jnp.concatenate([x[BASE[1] :], y[: PIECE[2]]]) for x, y in ((near0, later0), (near1, later1))]
     column = shifted(jnp.stack(column), (0, 0, 1), -1)
     part, column = lax.optimization_barrier((exchange(part, ("lat", "rep")), column))
-    mine = jnp.concatenate([part.reshape(1, GRAIN, 128), pack[:, GRAIN:]], axis=1)
+    mine = jnp.concatenate([part.reshape(1, GRAIN, 128), tables], axis=1)
     mine = exchange_columns(spread(mine, lax.axis_size("lon") // 2))
     return (mine, sibling(mine)), (near0, near1, later0, later1, column)
 

time: 142 us -> 142 us (level)
  no operation moved by 1% of the time
where the time goes in v1:
time: 142 us; the launch traced here: 141 us
  starting transfers between devices  47.7 us (34%)
  blocking collectives  39.4 us (28%)
  Pallas kernels  32.2 us (23%)
  waiting for transfers between devices  15.2 us (11%)
  local copies, waits for them, and re-layouts  4.57 us (3%)
    all_to_all x2, blocking collectives, exchange_columns(): lax.all_to_all(lax.optimization_barrier(x), 'lon', 0, 0, axis_index_group...  39.4 us
    pallas_call x7, Pallas kernels, run(): pl.pallas_call(kernel, out_shape=[jax.ShapeDtypeStruct(s, d) for s, d in...  32.2 us
    ppermute x15, starting transfers between devices, shifted(): return lax.ppermute(x, tuple(names), pairs)  30 us
    ppermute x15, waiting for transfers between devices, shifted(): return lax.ppermute(x, tuple(names), pairs)  10.3 us
    ppermute x3, starting transfers between devices, sibling(): lax.ppermute(x, 'lon', [(i, i ^ 1) for i in range(lax.axis_size('lon'))])  9.13 us
    all_to_all x2, starting transfers between devices, exchange(): return lax.all_to_all(lax.optimization_barrier(x), axes, 0, 0, tiled=True)  8.58 us
    unnamed x24, local copies, waits for them, and re-layouts  3.72 us
  transfers between devices with their start and end apart: 20, of which 7 were waited for; matrix products, arithmetic and copies ran while one was open for 0% of the time, Pallas kernels for 13%

profile of v1, /device:TPU:1, one launch (start us, length us, event | category | flops | bytes accessed | tf_op | source)
XLA Modules:
  0.0 141.4 jit_solution(10904423714593591464)
XLA Ops:
  0.6 6.5 %collective-permute-start.7 = (f32[1,2,6,3312]{3,1,2,0:T(2,128)}, f32[1,2,6,3312]{3,1,2,0:T(2,128)S(1)}, u32[]{:S(2)}, u32[]{:S(2)}) collective-permute-start(f32[1,2,6,3312]{3,1,2,0:T(2,128)} %param.16), channel_id=1, source_target_pairs={{0,14},{2,0},{4,2},{6,4},{8,6},{10,8},{12,10},{14,12},{1,15},{3,1}... | collective-permute-start | bytes 476936 | tf_op jit(solution)/shard_map/ppermute | solution.py:758
  11.4 5.5 %collective-permute-start.2 = (bf16[336,128]{1,0:T(8,128)(2,1)S(1)}, bf16[336,128]{1,0:T(8,128)(2,1)S(1)}, u32[]{:S(2)}, u32[]{:S(2)}) collective-permute-start(bf16[336,128]{1,0:T(8,128)(2,1)S(1)} %get-tuple-element.70), channel_id=1, source_target_pairs={{0,254},{2,240},{4,242},{6,244},{8,246},{10,248},{12,250},{14,252}... | collective-permute-start | bytes 258056 | tf_op jit(solution)/shard_map/ppermute | solution.py:758
  17.3 1.8 %collective-permute-start.4 = (bf16[336,128]{1,0:T(8,128)(2,1)S(1)}, bf16[336,128]{1,0:T(8,128)(2,1)S(1)}, u32[]{:S(2)}, u32[]{:S(2)}) collective-permute-start(bf16[336,128]{1,0:T(8,128)(2,1)S(1)} %get-tuple-element.72), channel_id=1, source_target_pairs={{0,241},{1,240},{16,1},{17,0},{32,17},{33,16},{48,33},{49,32},{64,... | collective-permute-start | bytes 258056 | tf_op jit(solution)/shard_map/ppermute | solution.py:758
  19.9 5.2 %collective-permute-start.6 = (bf16[336,128]{1,0:T(8,128)(2,1)S(1)}, bf16[336,128]{1,0:T(8,128)(2,1)S(1)}, u32[]{:S(2)}, u32[]{:S(2)}) collective-permute-start(bf16[336,128]{1,0:T(8,128)(2,1)S(1)} %get-tuple-element.74), channel_id=1, source_target_pairs={{0,255},{1,254},{2,241},{3,240},{4,243},{5,242},{6,245},{7,244},{8... | collective-permute-start | bytes 258056 | tf_op jit(solution)/shard_map/ppermute | solution.py:758
  27.0 3.3 %shard_map.212 = (f32[3,2,872,128]{3,2,1,0:T(8,128)S(1)}, f32[1,2,1736,128]{3,2,1,0:T(8,128)S(1)}) custom-call(f32[6,2,3312]{2,1,0:T(2,128)S(1)} %bitcast.26, f32[6,2,3312]{2,1,0:T(2,128)S(1)} %bitcast.28, f32[12,1,3312]{2,1,0:T(1,128)S(1)} %bitcast.27), custom_call_target="tpu_custom_call" | custom-call | flops 4294967296 | tf_op jit(solution)/shard_map/pallas_call | solution.py:738
  30.4 11.2 %shard_map.213 = (bf16[4,144,192]{2,1,0:T(8,128)(2,1)S(1)}, bf16[4,144,192]{2,1,0:T(8,128)(2,1)S(1)}, bf16[192,192]{1,0:T(8,128)(2,1)S(1)}, bf16[160,192]{1,0:T(...) custom-call(bf16[336,128]{1,0:T(8,128)(2,1)S(1)} %get-tuple-element., ...), custom_call_target="tpu_custom_call" | custom-call | flops 17179869184 | tf_op jit(solution)/shard_map/pallas_call | solution.py:738
  42.8 2.9 %shard_map.214 = (bf16[144,384]{1,0:T(8,128)(2,1)S(1)}, bf16[8,432,128]{2,1,0:T(8,128)(2,1)S(1)}, bf16[8,432,128]{2,1,0:T(8,128)(2,1)S(1)}, f32[16,3456]{1,0:T(8,128)S(1)}) custom-call(bf16[144,384]{1,0:T(8,128)(2,1)S(1)} %get-tuple-element.81.cin_ref, bf16[144,384]{1,0:T(8,128)(2,1)S(1)} %get-tuple-element.82.gy_ref, ...), custom_call_target="tpu_custom_call" | custom-call | flops 34359738368 | tf_op jit(solution)/shard_map/pallas_call | solution.py:738
  47.9 10.4 %shard_map.215 = (bf16[336,192]{1,0:T(8,128)(2,1)S(1)}, bf16[192,192]{1,0:T(8,128)(2,1)S(1)}, bf16[336,192]{1,0:T(8,128)(2,1)S(1)}, bf16[192,192]{1,0:T(8,128)(2...) custom-call(bf16[4,144,192]{2,1,0:T(8,128)(2,1)S(1)} %get-tuple-element.77.x_in, ...), custom_call_target="tpu_custom_call" | custom-call | flops 8589934592 | tf_op jit(solution)/shard_map/pallas_call | solution.py:738
  58.3 3.2 %collective-permute-start.12 = (bf16[8,144,128]{2,1,0:T(8,128)(2,1)S(1)}, bf16[8,144,128]{2,1,0:T(8,128)(2,1)S(1)}, u32[]{:S(2)}, u32[]{:S(2)}) collective-permute-start(bf16[8,144,128]{2,1,0:T(8,128)(2,1)S(1)} %get-tuple-element.96), channel_id=1, source_target_pairs={{0,16},{16,0},{32,48},{48,32},{64,80},{80,64},{96,112},{112,96},{1... | collective-permute-start | bytes 884744 | tf_op jit(solution)/shard_map/ppermute | solution.py:777
  61.5 1.2 collective-permute-done.12
  63.2 21.0 %all_to_all.20 = bf16[8,576,128]{2,1,0:T(8,128)(2,1)S(1)} all-to-all(bf16[8,576,128]{2,1,0:T(8,128)(2,1)S(1)} %pad_maximum_fusion), channel_id=1, replica_groups={{0,32,64,96,128,160,192,224},{16,48,80,112,144,176,208,240},{1,33,65,97..., dimensions={0} | all-to-all | bytes 2359296 | tf_op jit(solution)/shard_map/all_to_all | solution.py:783
  85.0 3.5 %all-to-all-start.1 = ((bf16[16,32,128]{2,1,0:T(8,128)(2,1)}), bf16[16,32,128]{2,1,0:T(8,128)(2,1)S(1)}, u32[]{:S(2)}, u32[]{:S(2)}) async-start(bf16[16,32,128]{2,1,0:T(8,128)(2,1)} %bitcast.7), calls=%async_computation.1 | async-start | bytes 262144 | tf_op jit(solution)/shard_map/all_to_all | solution.py:765
  88.5 1.2 collective-permute-start.13
  89.8 1.2 collective-permute-start.14
  92.2 3.3 %collective-permute-done.14.later0_ref = bf16[192,192]{1,0:T(8,128)(2,1)S(1)} collective-permute-done((bf16[192,192]{1,0:T(8,128)(2,1)S(1)}, bf16[192,192]{1,0:T(8,128)(2,1)S(1)}, u32[]{:S(2)}, u32[]{:S(2)}) %collective-permute-start.14) | collective-permute-done | bytes 73760 | tf_op jit(solution)/shard_map/ppermute | solution.py:758
  95.5 3.2 %collective-permute-done.15.later1_ref = bf16[192,192]{1,0:T(8,128)(2,1)S(1)} collective-permute-done((bf16[192,192]{1,0:T(8,128)(2,1)S(1)}, bf16[192,192]{1,0:T(8,128)(2,1)S(1)}, u32[]{:S(2)}, u32[]{:S(2)}) %collective-permute-start.15) | collective-permute-done | bytes 73760 | tf_op jit(solution)/shard_map/ppermute | solution.py:758
  99.4 5.1 %all-to-all-start.2 = ((bf16[16,32,128]{2,1,0:T(8,128)(2,1)}), bf16[16,32,128]{2,1,0:T(8,128)(2,1)S(1)}, u32[]{:S(2)}, u32[]{:S(2)}) async-start(bf16[16,32,128]{2,1,0:T(8,128)(2,1)} %broadcast_in_dim.8), calls=%async_computation.2 | async-start | bytes 262144 | tf_op jit(solution)/shard_map/all_to_all | solution.py:765
  104.6 3.3 %collective-permute-start.16 = (bf16[2,192,192]{2,1,0:T(8,128)(2,1)S(1)}, bf16[2,192,192]{2,1,0:T(8,128)(2,1)S(1)}, u32[]{:S(2)}, u32[]{:S(2)}) collective-permute-start(bf16[2,192,192]{2,1,0:T(8,128)(2,1)S(1)} %pad_maximum_fusion.1), channel_id=1, source_target_pairs={{0,16},{16,32},{32,48},{48,64},{64,80},{80,96},{96,112},{112,128},... | collective-permute-start | bytes 442376 | tf_op jit(solution)/shard_map/ppermute | solution.py:758
  107.9 2.6 %collective-permute-done.16.lon_ref = bf16[2,192,192]{2,1,0:T(8,128)(2,1)S(1)} collective-permute-done((bf16[2,192,192]{2,1,0:T(8,128)(2,1)S(1)}, bf16[2,192,192]{2,1,0:T(8,128)(2,1)S(1)}, u32[]{:S(2)}, u32[]{:S(2)}) %collective-permute-start.16) | collective-permute-done | bytes 147488 | tf_op jit(solution)/shard_map/ppermute | solution.py:758
  110.5 2.6 %all-to-all-done.2 = bf16[16,32,128]{2,1,0:T(8,128)(2,1)S(1)} async-done(((bf16[16,32,128]{2,1,0:T(8,128)(2,1)}), bf16[16,32,128]{2,1,0:T(8,128)(2,1)S(1)}, u32[]{:S(2)}, u32[]{:S(2)}) %all-to-all-start.2) | async-done | bytes 131104 | tf_op jit(solution)/shard_map/all_to_all | solution.py:765
  113.3 18.3 %all_to_all.21.refs_0_ = bf16[8,576,128]{2,1,0:T(8,128)(2,1)S(1)} all-to-all(bf16[8,576,128]{2,1,0:T(8,128)(2,1)S(1)} %broadcast_in_dim.20), channel_id=1, replica_groups={{0,32,64,96,128,160,192,224},{16,48,80,112,144,176,208,240},{1,33,65,97..., dimensions={0} | all-to-all | bytes 2359296 | tf_op jit(solution)/shard_map/all_to_all | solution.py:783
  131.7 4.9 %collective-permute-start.17 = (bf16[8,576,128]{2,1,0:T(8,128)(2,1)S(1)}, bf16[8,576,128]{2,1,0:T(8,128)(2,1)S(1)}, u32[]{:S(2)}, u32[]{:S(2)}) collective-permute-start(bf16[8,576,128]{2,1,0:T(8,128)(2,1)S(1)} %all_to_all.21.refs_0_), channel_id=1, source_target_pairs={{0,16},{16,0},{32,48},{48,32},{64,80},{80,64},{96,112},{112,96},{1... | collective-permute-start | bytes 3538952 | tf_op jit(solution)/shard_map/ppermute | solution.py:777
  136.5 1.5 %shard_map.216 = (bf16[2,12,24,192]{3,2,1,0:T(8,128)(2,1)}, bf16[6,12,2,384]{3,2,1,0:T(2,128)(2,1)}) custom-call(bf16[336,192]{1,0:T(8,128)(2,1)S(1)} %get-tuple-element.92.near0_ref, bf16[336,192]{1,0:T(8,128)(2,1)S(1)} %collective-permute-done.13.near1_ref, bf16[192,192]{1,0:T(8,128)(2,1)S(1)} %collective-permute-done.14.later0_ref, ...), custom_call_target="tpu_custom_call" | custom-call | tf_op jit(solution)/shard_map/pallas_call | solution.py:738
  139.0 2.4 %shard_map.217 = (f32[192]{0:T(256)}, f32[192,576]{1,0:T(8,128)}, f32[192,192]{1,0:T(8,128)}, f32[6,2,3312]{2,1,0:T(2,128)}, f32[768]{0:T(1024)}, /*index=5*/f32...) custom-call(bf16[8,576,128]{2,1,0:T(8,128)(2,1)S(1)} %all_to_all.21.refs_0_, ...), custom_call_target="tpu_custom_call" | custom-call | tf_op jit(solution)/shard_map/pallas_call | solution.py:738
  (64 shorter events, 15.1 us)
Async XLA Ops:
  0.6 19.2 %collective-permute-start.7 = (f32[1,2,6,3312]{3,1,2,0:T(2,128)}, f32[1,2,6,3312]{3,1,2,0:T(2,128)S(1)}, u32[]{:S(2)}, u32[]{:S(2)}) collective-permute-start(f32[1,2,6,3312]{3,1,2,0:T(2,128)} %param.16), channel_id=1, source_target_pairs={{0,14},{2,0},{4,2},{6,4},{8,6},{10,8},{12,10},{14,12},{1,15},{3,1}... | collective-permute-start | bytes 476936 | tf_op jit(solution)/shard_map/ppermute | solution.py:758
  9.7 7.6 %collective-permute-start = (bf16[336,128]{1,0:T(8,128)(2,1)S(1)}, bf16[336,128]{1,0:T(8,128)(2,1)S(1)}, u32[]{:S(2)}, u32[]{:S(2)}) collective-permute-start(bf16[336,128]{1,0:T(8,128)(2,1)S(1)} %get-tuple-element.68), channel_id=1, source_target_pairs={{0,240},{16,0},{32,16},{48,32},{64,48},{80,64},{96,80},{112,96},{1... | collective-permute-start | bytes 258056 | tf_op jit(solution)/shard_map/ppermute | solution.py:758
  10.7 8.4 %collective-permute-start.1 = (bf16[336,128]{1,0:T(8,128)(2,1)S(1)}, bf16[336,128]{1,0:T(8,128)(2,1)S(1)}, u32[]{:S(2)}, u32[]{:S(2)}) collective-permute-start(bf16[336,128]{1,0:T(8,128)(2,1)S(1)} %get-tuple-element.69), channel_id=1, source_target_pairs={{0,14},{2,0},{4,2},{6,4},{8,6},{10,8},{12,10},{14,12},{1,15},{3,1}... | collective-permute-start | bytes 258056 | tf_op jit(solution)/shard_map/ppermute | solution.py:758
  11.4 18.9 %collective-permute-start.2 = (bf16[336,128]{1,0:T(8,128)(2,1)S(1)}, bf16[336,128]{1,0:T(8,128)(2,1)S(1)}, u32[]{:S(2)}, u32[]{:S(2)}) collective-permute-start(bf16[336,128]{1,0:T(8,128)(2,1)S(1)} %get-tuple-element.70), channel_id=1, source_target_pairs={{0,254},{2,240},{4,242},{6,244},{8,246},{10,248},{12,250},{14,252}... | collective-permute-start | bytes 258056 | tf_op jit(solution)/shard_map/ppermute | solution.py:758
  17.0 13.3 %collective-permute-start.3 = (bf16[336,128]{1,0:T(8,128)(2,1)S(1)}, bf16[336,128]{1,0:T(8,128)(2,1)S(1)}, u32[]{:S(2)}, u32[]{:S(2)}) collective-permute-start(bf16[336,128]{1,0:T(8,128)(2,1)S(1)} %get-tuple-element.71), channel_id=1, source_target_pairs={{0,1},{1,0},{2,3},{3,2},{4,5},{5,4},{6,7},{7,6},{8,9},{9,8},{10,11... | collective-permute-start | bytes 258056 | tf_op jit(solution)/shard_map/ppermute | solution.py:758
  17.3 13.0 %collective-permute-start.4 = (bf16[336,128]{1,0:T(8,128)(2,1)S(1)}, bf16[336,128]{1,0:T(8,128)(2,1)S(1)}, u32[]{:S(2)}, u32[]{:S(2)}) collective-permute-start(bf16[336,128]{1,0:T(8,128)(2,1)S(1)} %get-tuple-element.72), channel_id=1, source_target_pairs={{0,241},{1,240},{16,1},{17,0},{32,17},{33,16},{48,33},{49,32},{64,... | collective-permute-start | bytes 258056 | tf_op jit(solution)/shard_map/ppermute | solution.py:758
  19.1 11.2 %collective-permute-start.5 = (bf16[336,128]{1,0:T(8,128)(2,1)S(1)}, bf16[336,128]{1,0:T(8,128)(2,1)S(1)}, u32[]{:S(2)}, u32[]{:S(2)}) collective-permute-start(bf16[336,128]{1,0:T(8,128)(2,1)S(1)} %get-tuple-element.73), channel_id=1, source_target_pairs={{0,15},{1,14},{2,1},{3,0},{4,3},{5,2},{6,5},{7,4},{8,7},{9,6},{10,... | collective-permute-start | bytes 258056 | tf_op jit(solution)/shard_map/ppermute | solution.py:758
  19.9 10.5 %collective-permute-start.6 = (bf16[336,128]{1,0:T(8,128)(2,1)S(1)}, bf16[336,128]{1,0:T(8,128)(2,1)S(1)}, u32[]{:S(2)}, u32[]{:S(2)}) collective-permute-start(bf16[336,128]{1,0:T(8,128)(2,1)S(1)} %get-tuple-element.74), channel_id=1, source_target_pairs={{0,255},{1,254},{2,241},{3,240},{4,243},{5,242},{6,245},{7,244},{8... | collective-permute-start | bytes 258056 | tf_op jit(solution)/shard_map/ppermute | solution.py:758
  27.0 3.4 %copy-start.5 = (bf16[192,576]{1,0:T(8,128)(2,1)S(1)}, bf16[192,576]{1,0:T(8,128)(2,1)}, u32[]{:S(2)}) copy-start(bf16[192,576]{1,0:T(8,128)(2,1)} %fqkv_ref.3) | copy-start | bytes 663556
  27.0 3.4 %copy-start.8 = (bf16[192,192]{1,0:T(8,128)(2,1)S(1)}, bf16[192,192]{1,0:T(8,128)(2,1)}, u32[]{:S(2)}) copy-start(bf16[192,192]{1,0:T(8,128)(2,1)} %fproj_ref.3) | copy-start | bytes 221188
  27.0 3.4 %copy-start.9 = (f32[768]{0:T(1024)S(1)}, f32[768]{0:T(1024)}, u32[]{:S(2)}) copy-start(f32[768]{0:T(1024)} %mgain_ref.1) | copy-start | bytes 9220
  27.0 3.4 %copy-start.10 = (f32[384]{0:T(512)S(1)}, f32[384]{0:T(512)}, u32[]{:S(2)}) copy-start(f32[384]{0:T(512)} %cgain_ref.1) | copy-start | bytes 4612
  41.6 6.3 %collective-permute-start.10 = (bf16[160,192]{1,0:T(8,128)(2,1)S(1)}, bf16[160,192]{1,0:T(8,128)(2,1)S(1)}, u32[]{:S(2)}, u32[]{:S(2)}) collective-permute-start(bf16[160,192]{1,0:T(8,128)(2,1)S(1)} %get-tuple-element.80), channel_id=1, source_target_pairs={{0,18},{2,20},{4,22},{6,24},{8,26},{10,28},{12,30},{14,16},{16,34}... | collective-permute-start | bytes 184328 | tf_op jit(solution)/shard_map/ppermute | solution.py:758
  41.7 6.2 %collective-permute-start.9 = (bf16[160,192]{1,0:T(8,128)(2,1)S(1)}, bf16[160,192]{1,0:T(8,128)(2,1)S(1)}, u32[]{:S(2)}, u32[]{:S(2)}) collective-permute-start(bf16[160,192]{1,0:T(8,128)(2,1)S(1)} %get-tuple-element.80), channel_id=1, source_target_pairs={{0,16},{16,32},{32,48},{48,64},{64,80},{80,96},{96,112},{112,128},... | collective-permute-start | bytes 184328 | tf_op jit(solution)/shard_map/ppermute | solution.py:758
  41.8 6.1 %collective-permute-start.8 = (bf16[192,192]{1,0:T(8,128)(2,1)S(1)}, bf16[192,192]{1,0:T(8,128)(2,1)S(1)}, u32[]{:S(2)}, u32[]{:S(2)}) collective-permute-start(bf16[192,192]{1,0:T(8,128)(2,1)S(1)} %get-tuple-element.79), channel_id=1, source_target_pairs={{0,2},{2,4},{4,6},{6,8},{8,10},{10,12},{12,14},{14,0},{1,3},{3,5},... | collective-permute-start | bytes 221192 | tf_op jit(solution)/shard_map/ppermute | solution.py:758
  45.7 17.1 %collective-permute-start.11 = (bf16[8,432,128]{2,1,0:T(8,128)(2,1)S(1)}, bf16[8,432,128]{2,1,0:T(8,128)(2,1)S(1)}, u32[]{:S(2)}, u32[]{:S(2)}) collective-permute-start(bf16[8,432,128]{2,1,0:T(8,128)(2,1)S(1)} %get-tuple-element.95), channel_id=1, source_target_pairs={{0,16},{16,0},{32,48},{48,32},{64,80},{80,64},{96,112},{112,96},{1... | collective-permute-start | bytes 2654216 | tf_op jit(solution)/shard_map/ppermute | solution.py:777
  58.3 4.4 %collective-permute-start.12 = (bf16[8,144,128]{2,1,0:T(8,128)(2,1)S(1)}, bf16[8,144,128]{2,1,0:T(8,128)(2,1)S(1)}, u32[]{:S(2)}, u32[]{:S(2)}) collective-permute-start(bf16[8,144,128]{2,1,0:T(8,128)(2,1)S(1)} %get-tuple-element.96), channel_id=1, source_target_pairs={{0,16},{16,0},{32,48},{48,32},{64,80},{80,64},{96,112},{112,96},{1... | collective-permute-start | bytes 884744 | tf_op jit(solution)/shard_map/ppermute | solution.py:777
  85.0 13.7 %all-to-all-start.1 = ((bf16[16,32,128]{2,1,0:T(8,128)(2,1)}), bf16[16,32,128]{2,1,0:T(8,128)(2,1)S(1)}, u32[]{:S(2)}, u32[]{:S(2)}) async-start(bf16[16,32,128]{2,1,0:T(8,128)(2,1)} %bitcast.7), calls=%async_computation.1 | async-start | bytes 262144 | tf_op jit(solution)/shard_map/all_to_all | solution.py:765
  88.5 10.2 %collective-permute-start.13 = (bf16[336,192]{1,0:T(8,128)(2,1)S(1)}, bf16[336,192]{1,0:T(8,128)(2,1)S(1)}, u32[]{:S(2)}, u32[]{:S(2)}) collective-permute-start(bf16[336,192]{1,0:T(8,128)(2,1)S(1)} %get-tuple-element.101), channel_id=1, source_target_pairs={{0,1},{1,0},{2,3},{3,2},{4,5},{5,4},{6,7},{7,6},{8,9},{9,8},{10,11... | collective-permute-start | bytes 387080 | tf_op jit(solution)/shard_map/ppermute | solution.py:758
  89.8 5.7 %collective-permute-start.14 = (bf16[192,192]{1,0:T(8,128)(2,1)S(1)}, bf16[192,192]{1,0:T(8,128)(2,1)S(1)}, u32[]{:S(2)}, u32[]{:S(2)}) collective-permute-start(bf16[192,192]{1,0:T(8,128)(2,1)S(1)} %get-tuple-element.102), channel_id=1, source_target_pairs={{0,2},{2,4},{4,6},{6,8},{8,10},{10,12},{12,14},{14,0},{1,3},{3,5},... | collective-permute-start | bytes 221192 | tf_op jit(solution)/shard_map/ppermute | solution.py:758
  91.0 7.7 %collective-permute-start.15 = (bf16[192,192]{1,0:T(8,128)(2,1)S(1)}, bf16[192,192]{1,0:T(8,128)(2,1)S(1)}, u32[]{:S(2)}, u32[]{:S(2)}) collective-permute-start(bf16[192,192]{1,0:T(8,128)(2,1)S(1)} %get-tuple-element.103), channel_id=1, source_target_pairs={{0,3},{1,2},{2,5},{3,4},{4,7},{5,6},{6,9},{7,8},{8,11},{9,10},{10,... | collective-permute-start | bytes 221192 | tf_op jit(solution)/shard_map/ppermute | solution.py:758
  99.4 13.7 %all-to-all-start.2 = ((bf16[16,32,128]{2,1,0:T(8,128)(2,1)}), bf16[16,32,128]{2,1,0:T(8,128)(2,1)S(1)}, u32[]{:S(2)}, u32[]{:S(2)}) async-start(bf16[16,32,128]{2,1,0:T(8,128)(2,1)} %broadcast_in_dim.8), calls=%async_computation.2 | async-start | bytes 262144 | tf_op jit(solution)/shard_map/all_to_all | solution.py:765
  104.6 5.9 %collective-permute-start.16 = (bf16[2,192,192]{2,1,0:T(8,128)(2,1)S(1)}, bf16[2,192,192]{2,1,0:T(8,128)(2,1)S(1)}, u32[]{:S(2)}, u32[]{:S(2)}) collective-permute-start(bf16[2,192,192]{2,1,0:T(8,128)(2,1)S(1)} %pad_maximum_fusion.1), channel_id=1, source_target_pairs={{0,16},{16,32},{32,48},{48,64},{64,80},{80,96},{96,112},{112,128},... | collective-permute-start | bytes 442376 | tf_op jit(solution)/shard_map/ppermute | solution.py:758
  131.7 7.3 %collective-permute-start.17 = (bf16[8,576,128]{2,1,0:T(8,128)(2,1)S(1)}, bf16[8,576,128]{2,1,0:T(8,128)(2,1)S(1)}, u32[]{:S(2)}, u32[]{:S(2)}) collective-permute-start(bf16[8,576,128]{2,1,0:T(8,128)(2,1)S(1)} %all_to_all.21.refs_0_), channel_id=1, source_target_pairs={{0,16},{16,0},{32,48},{48,32},{64,80},{80,64},{96,112},{112,96},{1... | collective-permute-start | bytes 3538952 | tf_op jit(solution)/shard_map/ppermute | solution.py:777
  (8 other events, 17.3 us)
